TPU v7x, 32 devices: a whole 2x2x4 slice. The times are simulated.
32 devices in a mesh: row: 4 (over y, core), col: 8 (over z, x).
Axes of the slice: x: 2, y: 2, z: 4, core: 2. Of those that a mesh axis runs over, the one named last changes fastest.
Arguments:
- trailing: bfloat16 [4096, 4096], P('row', 'col'), may hold values from -6 to 6
- left_outer: bfloat16 [384, 4096], P('col', 'row'), may hold values from -0.625 to 0.625
- left_inner: bfloat16 [384, 4096], P('col', 'row'), may hold values from -0.1875 to 0.1875
- upper_outer: bfloat16 [384, 4096], P('row', 'col'), may hold values from -6 to 6
- upper_inner: bfloat16 [384, 4096], P('row', 'col'), may hold values from -0.3125 to 0.3125
- left_ranks: int32 [4, 4], replicated, may hold values from 16 to 96
- upper_ranks: int32 [4, 4], replicated, may hold values from 16 to 96
Outputs:
- updated: bfloat16 [4096, 4096], P('row', 'col')
- next_panel: bfloat16 [4096, 1024], P(('row', 'col'))
All inputs are finite; a program needn't handle non-finite values.
Results may differ from a plain program's by a relative error of at most 0.0042.
Values may be sent and summed in bfloat16 or wider, within the bound.
A program may use at most 64 MiB of HBM per device.

v0:
```python
import jax
import jax.numpy as jnp
from jax import lax
from jax.sharding import PartitionSpec as P

R = 96


def partner_2(block, axis, stride):
    count = lax.axis_size(axis)
    route = []
    for low in range(count):
        high = low | 1 << stride
        if high != low and high < count:
            route += [(low, high), (high, low)]
    return lax.ppermute(block, axis, route)


def passed_along(value, axis, steps):
    count = lax.axis_size(axis)
    pairs = [(source, (source + steps) % count) for source in range(count)]
    return lax.ppermute(value, axis, pairs)


def from_root(block, axis, source):
    block = jnp.where(lax.axis_index(axis) == source, block, jnp.zeros_like(block))
    return lax.psum(block, axis)


def body(trailing, left_outer, left_inner, upper_outer, upper_inner, left_ranks, upper_ranks):
    half_rank = R // 2
    row_at = lax.axis_index("row")
    col_at = lax.axis_index("col")
    column_count = lax.axis_size("col")
    tile_count = lax.axis_size("row")
    own_tile = col_at // 2
    partner = partner_2(upper_outer, "col", 0)
    even_side = col_at % 2 == 0
    lower_half = jnp.where(even_side, upper_outer, partner)
    top_half_block = jnp.where(even_side, partner, upper_outer)
    top_rows = jnp.concatenate([lower_half, top_half_block], axis=1)
    all_rows, every_column = (
        lax.all_gather(top_rows, "row", axis=0, tiled=True),
        lax.all_gather(upper_inner, "row", axis=0, tiled=True),
    )
    rank_index = jnp.arange(R, dtype=jnp.int32)
    col_ranks = lax.dynamic_index_in_dim(upper_ranks, own_tile, 1, keepdims=False)
    upper_live = rank_index[None, :] < col_ranks[:, None]
    row_ranks = lax.dynamic_index_in_dim(left_ranks, row_at, 0, keepdims=False)

    def contribute(buffer, outer_rows, interior_rows, first_row):
        row_count = outer_rows.shape[0]
        panel_at = first_row // R
        offset = first_row % R
        rank_here = lax.dynamic_index_in_dim(row_ranks, panel_at, 0, keepdims=False)
        upper_tile = lax.dynamic_slice_in_dim(all_rows, panel_at * R, R, 0)
        central_block = lax.dot_general(
            interior_rows, upper_tile, (((1,), (1,)), ((), ())), preferred_element_type=jnp.float32
        )
        live_rows = offset + jnp.arange(row_count, dtype=jnp.int32) < rank_here
        active_columns = lax.dynamic_index_in_dim(upper_live, panel_at, 0, keepdims=False)
        central_block = jnp.where(
            live_rows[:, None] & active_columns[None, :], central_block, 0.0
        ).astype(jnp.bfloat16)
        partial_value = lax.dot_general(
            outer_rows, central_block, (((0,), (0,)), ((), ())), preferred_element_type=jnp.float32
        )
        rank_slot = lax.dynamic_slice_in_dim(buffer, panel_at * R, R, 1)
        return lax.dynamic_update_slice_in_dim(buffer, rank_slot + partial_value, panel_at * R, 1)

    stacked = jnp.stack([left_outer, left_inner])
    buffer = jnp.zeros((trailing.shape[0], tile_count * R), jnp.float32)

    def advance(shift_step, carried_state):
        carried, block_parts = carried_state
        held_piece = (col_at - shift_step) % column_count
        carried = contribute(carried, block_parts[0], block_parts[1], held_piece * half_rank)
        block_parts = passed_along(block_parts, "col", 1)
        return (carried, block_parts)

    buffer, block_parts = lax.fori_loop(0, column_count - 1, advance, (buffer, stacked))
    held_piece = (col_at - (column_count - 1)) % column_count
    buffer = contribute(buffer, block_parts[0], block_parts[1], held_piece * half_rank)
    outer_sum = buffer.astype(jnp.bfloat16)
    product = jnp.dot(outer_sum, every_column, preferred_element_type=jnp.float32)
    updated = (trailing.astype(jnp.float32) - product).astype(jnp.bfloat16)
    received = []
    for which_half in range(2):
        received.append(from_root(updated, "col", which_half))
    whole_panel = jnp.concatenate(received, axis=1)
    share_rows = whole_panel.shape[0] // column_count
    next_panel = lax.dynamic_slice_in_dim(whole_panel, col_at * share_rows, share_rows, 0)
    return (updated, next_panel)


def solution(mesh):
    in_specs = (
        P("row", "col"),
        P("col", "row"),
        P("col", "row"),
        P("row", "col"),
        P("row", "col"),
        P(),
        P(),
    )
    out_specs = (P("row", "col"), P(("row", "col"), None))
    return jax.shard_map(body, mesh=mesh, in_specs=in_specs, out_specs=out_specs, check_vma=False)
```

profile of v0, /device:TPU:24, one launch (start us, length us, event | category | flops | bytes accessed | tf_op | source)
XLA Modules:
  0.0 201.4 jit_solution(15014900572631212373)
XLA Ops:
  7.2 1.6 collective-permute-start.1
  8.8 0.7 fusion.38
  9.7 6.7 %all_gather.7 = bf16[384,512]{1,0:T(8,128)(2,1)S(1)} all-gather(bf16[96,512]{1,0:T(8,128)(2,1)} %param.13), channel_id=1, replica_groups=mesh['row'=4,'col'=8] {'row'}, dimensions={0}, use_global_device_ids=true | all-gather | bytes 491520 | tf_op jit(solution)/shard_map/all_gather | solution.py:44
  16.4 1.3 dynamic_slice.72
  17.7 1.0 pad_maximum_fusion
  18.7 0.6 add_compare_fusion.1
  19.2 0.9 broadcast_select_fusion.3
  20.2 8.7 %all_gather.6 = bf16[384,1024]{1,0:T(8,128)(2,1)S(1)} all-gather(bf16[96,1024]{1,0:T(8,128)(2,1)S(1)} %pad_maximum_fusion.1), channel_id=1, replica_groups=mesh['row'=4,'col'=8] {'row'}, dimensions={0}, use_global_device_ids=true | all-gather | bytes 983040 | tf_op jit(solution)/shard_map/all_gather | solution.py:43
  29.1 53.1 %while.18 = (s32[]{:T(128)}, f32[1024,384]{0,1:T(8,128)S(1)}, bf16[2,48,1024]{2,1,0:T(8,128)(2,1)S(1)}, s32[]{:T(128)}, s32[4]{0:T(128)S(1)}, /*index=5*/pred[4,...) while((s32[]{:T(128)}, f32[1024,384]{0,1:T(8,128)S(1)}, ...), condition=%wide.region_1.2_spmd, body=%wide.region_0.1_spmd.sunk | while | flops 18986624 | bytes 2362125 | solution.py:81
  29.1 0.6 collective-permute-start
  29.7 0.6 dynamic_slice.107
  30.3 0.6 add_compare_fusion.3
  31.4 5.9 %collective-permute-done = bf16[2,48,1024]{2,1,0:T(8,128)(2,1)S(1)} collective-permute-done((bf16[2,48,1024]{2,1,0:T(8,128)(2,1)S(1)}, bf16[2,48,1024]{2,1,0:T(8,128)(2,1)S(1)}, u32[]{:S(2)}, u32[]{:S(2)}) %collective-permute-start) | collective-permute-done | bytes 196640 | tf_op jit(solution)/shard_map/while/body/eval_jaxpr/ppermute | solution.py:22
  37.4 0.6 dynamic_slice.107
  39.0 5.5 %collective-permute-done = bf16[2,48,1024]{2,1,0:T(8,128)(2,1)S(1)} collective-permute-done((bf16[2,48,1024]{2,1,0:T(8,128)(2,1)S(1)}, bf16[2,48,1024]{2,1,0:T(8,128)(2,1)S(1)}, u32[]{:S(2)}, u32[]{:S(2)}) %collective-permute-start) | collective-permute-done | bytes 196640 | tf_op jit(solution)/shard_map/while/body/eval_jaxpr/ppermute | solution.py:22
  44.7 0.6 dynamic_slice.107
  46.4 4.8 %collective-permute-done = bf16[2,48,1024]{2,1,0:T(8,128)(2,1)S(1)} collective-permute-done((bf16[2,48,1024]{2,1,0:T(8,128)(2,1)S(1)}, bf16[2,48,1024]{2,1,0:T(8,128)(2,1)S(1)}, u32[]{:S(2)}, u32[]{:S(2)}) %collective-permute-start) | collective-permute-done | bytes 196640 | tf_op jit(solution)/shard_map/while/body/eval_jaxpr/ppermute | solution.py:22
  51.2 2.0 collective-permute-start
  53.1 0.6 dynamic_slice.107
  54.8 3.0 %collective-permute-done = bf16[2,48,1024]{2,1,0:T(8,128)(2,1)S(1)} collective-permute-done((bf16[2,48,1024]{2,1,0:T(8,128)(2,1)S(1)}, bf16[2,48,1024]{2,1,0:T(8,128)(2,1)S(1)}, u32[]{:S(2)}, u32[]{:S(2)}) %collective-permute-start) | collective-permute-done | bytes 196640 | tf_op jit(solution)/shard_map/while/body/eval_jaxpr/ppermute | solution.py:22
  57.9 3.7 %collective-permute-start = (bf16[2,48,1024]{2,1,0:T(8,128)(2,1)S(1)}, bf16[2,48,1024]{2,1,0:T(8,128)(2,1)S(1)}, u32[]{:S(2)}, u32[]{:S(2)}) collective-permute-start(bf16[2,48,1024]{2,1,0:T(8,128)(2,1)S(1)} %copy.15), channel_id=1, source_target_pairs={{0,1},{1,2},{2,3},{3,4},{4,5},{5,6},{6,7},{7,0},{8,9},{9,10},{10,1... | collective-permute-start | bytes 589832 | tf_op jit(solution)/shard_map/while/body/eval_jaxpr/ppermute | solution.py:22
  61.6 0.6 dynamic_slice.107
  63.2 1.6 collective-permute-done
  64.8 5.2 %collective-permute-start = (bf16[2,48,1024]{2,1,0:T(8,128)(2,1)S(1)}, bf16[2,48,1024]{2,1,0:T(8,128)(2,1)S(1)}, u32[]{:S(2)}, u32[]{:S(2)}) collective-permute-start(bf16[2,48,1024]{2,1,0:T(8,128)(2,1)S(1)} %copy.15), channel_id=1, source_target_pairs={{0,1},{1,2},{2,3},{3,4},{4,5},{5,6},{6,7},{7,0},{8,9},{9,10},{10,1... | collective-permute-start | bytes 589832 | tf_op jit(solution)/shard_map/while/body/eval_jaxpr/ppermute | solution.py:22
  70.0 0.6 dynamic_slice.107
  71.7 1.8 collective-permute-done
  73.5 5.5 %collective-permute-start = (bf16[2,48,1024]{2,1,0:T(8,128)(2,1)S(1)}, bf16[2,48,1024]{2,1,0:T(8,128)(2,1)S(1)}, u32[]{:S(2)}, u32[]{:S(2)}) collective-permute-start(bf16[2,48,1024]{2,1,0:T(8,128)(2,1)S(1)} %copy.15), channel_id=1, source_target_pairs={{0,1},{1,2},{2,3},{3,4},{4,5},{5,6},{6,7},{7,0},{8,9},{9,10},{10,1... | collective-permute-start | bytes 589832 | tf_op jit(solution)/shard_map/while/body/eval_jaxpr/ppermute | solution.py:22
  79.0 0.6 dynamic_slice.107
  80.7 1.5 collective-permute-done
  82.7 3.8 %broadcast_select_fusion = (bf16[1024,512]{1,0:T(8,128)(2,1)}, bf16[1024,512]{1,0:T(8,128)(2,1)}, bf16[1024,512]{1,0:T(8,128)(2,1)}) fusion(pred[]{:T(512)S(6)} %eq.29, pred[]{:T(512)S(6)} %eq.28, bf16[384,512]{1,0:T(8,128)(2,1)S(1)} %all_gather.7, f32[1024,384]{0,1:T(8,128)S(1)} %fusion.19, bf16[1024,512]{1,0:T(8,128)(2,1)} %param.9), kind=kOutput, calls=%fused_computation.26 | convolution fusion | flops 405667840 | bytes 6160386 | tf_op jit(solution)/shard_map/dot_general | solution.py:85
  86.5 106.4 %all-reduce.3.cloned.1.call-done = (bf16[1024,512]{1,0:T(8,128)(2,1)}, bf16[1024,512]{1,0:T(8,128)(2,1)}) async-done(((bf16[1024,512]{1,0:T(8,128)(2,1)}, bf16[1024,512]{1,0:T(8,128)(2,1)}), (bf16[1024,512]{1,0:T(8,128)(2,1)}, bf16[1024,512]{1,0:T(8,128)(2,1)})) %all-reduce.3.cloned.1.call-update) | async-done | bytes 2097168 | tf_op jit(solution)/shard_map/psum | solution.py:27
  192.9 1.7 fusion.22
  (40 shorter events, 8.2 us)
Async XLA Ops:
  7.2 2.3 %copy-start = (s32[4,4]{1,0:T(4,128)S(1)}, s32[4,4]{1,0:T(4,128)}, u32[]{:S(2)}) copy-start(s32[4,4]{1,0:T(4,128)} %param.15) | copy-start | bytes 196
  7.2 185.7 %all-reduce.3.cloned.1.call-start = ((), (), s32[]{:S(2)}) async-start(), calls=%async_computation | async-start | bytes 4194304 | tf_op jit(solution)/shard_map/psum | solution.py:27
  7.2 12.0 %collective-permute-start.1 = (bf16[96,512]{1,0:T(8,128)(2,1)}, bf16[96,512]{1,0:T(8,128)(2,1)S(1)}, u32[]{:S(2)}, u32[]{:S(2)}) collective-permute-start(bf16[96,512]{1,0:T(8,128)(2,1)} %param.12), channel_id=1, source_target_pairs={{0,1},{1,0},{2,3},{3,2},{4,5},{5,4},{6,7},{7,6},{8,9},{9,8},{10,11... | collective-permute-start | bytes 294920 | tf_op jit(solution)/shard_map/ppermute | solution.py:16
  29.1 8.1 %collective-permute-start = (bf16[2,48,1024]{2,1,0:T(8,128)(2,1)S(1)}, bf16[2,48,1024]{2,1,0:T(8,128)(2,1)S(1)}, u32[]{:S(2)}, u32[]{:S(2)}) collective-permute-start(bf16[2,48,1024]{2,1,0:T(8,128)(2,1)S(1)} %copy.15), channel_id=1, source_target_pairs={{0,1},{1,2},{2,3},{3,4},{4,5},{5,6},{6,7},{7,0},{8,9},{9,10},{10,1... | collective-permute-start | bytes 589832 | tf_op jit(solution)/shard_map/while/body/eval_jaxpr/ppermute | solution.py:22
  37.2 7.3 %collective-permute-start = (bf16[2,48,1024]{2,1,0:T(8,128)(2,1)S(1)}, bf16[2,48,1024]{2,1,0:T(8,128)(2,1)S(1)}, u32[]{:S(2)}, u32[]{:S(2)}) collective-permute-start(bf16[2,48,1024]{2,1,0:T(8,128)(2,1)S(1)} %copy.15), channel_id=1, source_target_pairs={{0,1},{1,2},{2,3},{3,4},{4,5},{5,6},{6,7},{7,0},{8,9},{9,10},{10,1... | collective-permute-start | bytes 589832 | tf_op jit(solution)/shard_map/while/body/eval_jaxpr/ppermute | solution.py:22
  44.6 6.6 %collective-permute-start = (bf16[2,48,1024]{2,1,0:T(8,128)(2,1)S(1)}, bf16[2,48,1024]{2,1,0:T(8,128)(2,1)S(1)}, u32[]{:S(2)}, u32[]{:S(2)}) collective-permute-start(bf16[2,48,1024]{2,1,0:T(8,128)(2,1)S(1)} %copy.15), channel_id=1, source_target_pairs={{0,1},{1,2},{2,3},{3,4},{4,5},{5,6},{6,7},{7,0},{8,9},{9,10},{10,1... | collective-permute-start | bytes 589832 | tf_op jit(solution)/shard_map/while/body/eval_jaxpr/ppermute | solution.py:22
  51.2 6.7 %collective-permute-start = (bf16[2,48,1024]{2,1,0:T(8,128)(2,1)S(1)}, bf16[2,48,1024]{2,1,0:T(8,128)(2,1)S(1)}, u32[]{:S(2)}, u32[]{:S(2)}) collective-permute-start(bf16[2,48,1024]{2,1,0:T(8,128)(2,1)S(1)} %copy.15), channel_id=1, source_target_pairs={{0,1},{1,2},{2,3},{3,4},{4,5},{5,6},{6,7},{7,0},{8,9},{9,10},{10,1... | collective-permute-start | bytes 589832 | tf_op jit(solution)/shard_map/while/body/eval_jaxpr/ppermute | solution.py:22
  57.9 6.9 %collective-permute-start = (bf16[2,48,1024]{2,1,0:T(8,128)(2,1)S(1)}, bf16[2,48,1024]{2,1,0:T(8,128)(2,1)S(1)}, u32[]{:S(2)}, u32[]{:S(2)}) collective-permute-start(bf16[2,48,1024]{2,1,0:T(8,128)(2,1)S(1)} %copy.15), channel_id=1, source_target_pairs={{0,1},{1,2},{2,3},{3,4},{4,5},{5,6},{6,7},{7,0},{8,9},{9,10},{10,1... | collective-permute-start | bytes 589832 | tf_op jit(solution)/shard_map/while/body/eval_jaxpr/ppermute | solution.py:22
  64.8 8.6 %collective-permute-start = (bf16[2,48,1024]{2,1,0:T(8,128)(2,1)S(1)}, bf16[2,48,1024]{2,1,0:T(8,128)(2,1)S(1)}, u32[]{:S(2)}, u32[]{:S(2)}) collective-permute-start(bf16[2,48,1024]{2,1,0:T(8,128)(2,1)S(1)} %copy.15), channel_id=1, source_target_pairs={{0,1},{1,2},{2,3},{3,4},{4,5},{5,6},{6,7},{7,0},{8,9},{9,10},{10,1... | collective-permute-start | bytes 589832 | tf_op jit(solution)/shard_map/while/body/eval_jaxpr/ppermute | solution.py:22
  73.5 8.7 %collective-permute-start = (bf16[2,48,1024]{2,1,0:T(8,128)(2,1)S(1)}, bf16[2,48,1024]{2,1,0:T(8,128)(2,1)S(1)}, u32[]{:S(2)}, u32[]{:S(2)}) collective-permute-start(bf16[2,48,1024]{2,1,0:T(8,128)(2,1)S(1)} %copy.15), channel_id=1, source_target_pairs={{0,1},{1,2},{2,3},{3,4},{4,5},{5,6},{6,7},{7,0},{8,9},{9,10},{10,1... | collective-permute-start | bytes 589832 | tf_op jit(solution)/shard_map/while/body/eval_jaxpr/ppermute | solution.py:22
Sparse Core Ops, SparseCore 0:
  86.6 106.2 all-reduce.2
where the time goes:
time: 205 us; the launch traced here: 201 us
  waiting for transfers between devices  131 us (64%)
  starting transfers between devices  18.8 us (9%)
  blocking collectives  15.4 us (8%)
  between operations  14.1 us (7%)
  other arithmetic  8.16 us (4%)
  matrix products  7.77 us (4%)
  local copies, waits for them, and re-layouts  6.5 us (3%)
    psum x1, waiting for transfers between devices, from_root(): return lax.psum(block, axis)  106 us
    ppermute x7, waiting for transfers between devices, passed_along(): return lax.ppermute(value, axis, pairs)  24.1 us
    ppermute x7, starting transfers between devices, passed_along(): return lax.ppermute(value, axis, pairs)  17.2 us
    all_gather x1, blocking collectives, body(): lax.all_gather(top_rows, 'row', axis=0, tiled=True)  8.72 us
    all_gather x1, blocking collectives, body(): lax.all_gather(upper_inner, 'row', axis=0, tiled=True)  6.69 us
    dynamic_slice x8, local copies, waits for them, and re-layouts, contribute(): rank_here = lax.dynamic_index_in_dim(row_ranks, panel_at, 0, keepdims=False)  5.29 us
    lt x8, other arithmetic, contribute(): live_rows = offset + jnp.arange(row_count, dtype=jnp.int32) < rank_here  4.51 us
  transfers between devices with their start and end apart: 9, of which 8 were waited for; matrix products, arithmetic and copies ran while one was open for 8% of the time, Pallas kernels for 0%

commit v1 on v0

v1 whole, which is shorter than its diff:
```python
import functools

import jax
import jax.numpy as jnp
from jax import lax
from jax.experimental import pallas as pl
from jax.experimental.pallas import tpu as pltpu
from jax.sharding import PartitionSpec as P

MESH = pl.DeviceIdType.MESH
LANES = 128
F32 = jnp.float32
BF16 = jnp.bfloat16


def sem_names(n, nh):
    names = ["px", "x0", "q1", "p1", "z1", "zx", "zc", "cx", "c0", "c0x", "pfx"]
    for s in range(1, n):
        names += [f"xb{s}", f"xa{s}", f"yb{s}", f"ya{s}", f"cb{s}", f"ca{s}"]
        names += [f"fw{s}", f"ow{s}"]
    for d in range(1, nh):
        names += [f"p{a}{d}" for a in "ghijkl"]
    return {name: at for at, name in enumerate(names)}


def kernel(n, names, tr_in, x_in, y_in, p_in, q_in, lr, ur, up_out, np_out,
           xg, yg, pg, qg, q0g, cb, c0, og, og0, prod0, tr, ub, pf, pin, nb,
           ssem, rsem, lsem):
    nh = n // 2
    rank = p_in.shape[0]
    hr = x_in.shape[0]
    tile, width = tr_in.shape
    sr = np_out.shape[0]
    row, col = lax.axis_index("row"), lax.axis_index("col")
    zz, h = col // 2, col % 2
    oh = 1 - h
    hi, core = row // 2, row % 2
    mate = hi * 2 + (1 - core)
    xn = (row, zz * 2 + oh)
    up = (row, lax.rem(zz + 1, n) * 2 + h)
    down = (row, lax.rem(zz + n - 1, n) * 2 + h)
    first, rest = zz == 0, zz > 0
    has_up, has_down = zz < n - 1, zz > 0
    pending = []

    def on(cond, f):
        if cond is None:
            f()
        else:
            pl.when(cond)(f)

    def desc(name, src, dst, dev):
        at = names[name]
        return pltpu.make_async_remote_copy(
            src_ref=src(), dst_ref=dst(), send_sem=ssem.at[at], recv_sem=rsem.at[at],
            device_id=dev, device_id_type=MESH)

    def go(name, src, dst, dev, cond=None, sem=None):
        def make():
            at = names[sem or name]
            return pltpu.make_async_remote_copy(
                src_ref=src(), dst_ref=dst(), send_sem=ssem.at[names[name]],
                recv_sem=rsem.at[at], device_id=dev, device_id_type=MESH)
        on(cond, lambda: make().start())
        pending.append((cond, lambda: make().wait_send()))

    def got(name, dst, cond=None):
        on(cond, lambda: desc(name, dst, dst, xn).wait_recv())

    def local(at, src, dst, cond=None):
        def make():
            return pltpu.make_async_copy(src(), dst(), lsem.at[at])
        on(cond, lambda: make().start())
        return lambda: on(cond, lambda: make().wait())

    partners = [xn, (mate, col)]
    for s in range(1, n):
        partners.append((row, lax.rem(zz + s, n) * 2 + h))
    for d in range(1, nh):
        partners.append((lax.rem(hi + d, nh) * 2 + core, col))
    barrier = pltpu.get_barrier_semaphore()
    for dev in partners:
        pl.semaphore_signal(barrier, inc=1, device_id=dev, device_id_type=MESH)
    pl.semaphore_wait(barrier, len(partners))

    def ref(r):
        return lambda: r

    pd = pl.ds(0, rank)
    for nm, src, dst in (("y", y_in, lambda k: yg.at[k]), ("x", x_in, lambda k: xg.at[k, h])):
        go(nm + "b1", ref(src), lambda dst=dst: dst(zz), up, has_up)
        go(nm + "a1", ref(src), lambda dst=dst: dst(zz), down, has_down)
    go("px", ref(p_in), lambda: pg.at[row, h, pd], xn)
    go("x0", ref(x_in), lambda: xg.at[zz, h], xn)
    go("z1", ref(q_in), lambda: q0g.at[row, h, pd], up, first)
    go("zx", ref(q_in), lambda: q0g.at[row, h, pd], xn, first)
    go("q1", ref(q_in), lambda: qg.at[row, pd], (mate, col))
    for d in range(1, nh):
        go(f"pg{d}", ref(q_in), lambda: qg.at[row, pd], (lax.rem(hi + d, nh) * 2 + core, col))
    w_p = local(0, ref(p_in), lambda: pg.at[row, h, pd])
    w_x = local(1, ref(x_in), lambda: xg.at[zz, h])
    w_y = local(2, ref(y_in), lambda: yg.at[zz])
    w_q = local(3, ref(q_in), lambda: qg.at[row, pd])
    w_q0 = local(4, ref(q_in), lambda: q0g.at[row, h, pd], first)

    def rows_of(z, side):
        return pl.ds(pl.multiple_of((z * 2 + side) * sr, sr), sr)

    go("pfx", lambda: tr_in.at[rows_of(0, oh)], lambda: pin.at[h], xn, first)
    for s in range(n - 1, 0, -1):
        go(f"fw{s}", lambda s=s: tr_in.at[rows_of(s, oh)], ref(pf), (row, s * 2 + h), first, "fw1")
    for s in range(n - 1, 0, -1):
        go(f"ow{s}", lambda s=s: tr_in.at[rows_of(s, h)], lambda: pin.at[h], (row, s * 2 + h), first, "ow1")
    w_pin = local(5, lambda: tr_in.at[rows_of(0, h)], lambda: pin.at[h], first)
    w_tr = local(6, ref(tr_in), ref(tr))

    pad = LANES - rank
    pg[:, :, rank:, :] = jnp.zeros((n, 2, pad, width), BF16)
    qg[:, rank:, :] = jnp.zeros((n, pad, width), BF16)
    q0g[:, :, rank:, :] = jnp.zeros((n, 2, pad, width), BF16)

    w_p()
    got("px", lambda: pg.at[row, oh, pd])
    go("p1", lambda: pg.at[row, :, pd], lambda: pg.at[row, :, pd], (mate, col))
    for d in range(1, nh):
        go(f"ph{d}", lambda: pg.at[row, :, pd], lambda: pg.at[row, :, pd],
           (lax.rem(hi + d, nh) * 2 + core, col))

    def relay(s):
        for side, dev, ok, more, slot in (
            ("b", up, zz - s >= 0, (zz - s >= 0) & has_up, lax.rem(zz - s + n, n)),
            ("a", down, zz + s < n, (zz + s < n) & has_down, lax.rem(zz + s, n)),
        ):
            for nm, dst in (("y", lambda slot=slot: yg.at[slot]), ("x", lambda slot=slot: xg.at[slot, h])):
                got(f"{nm}{side}{s}", dst, ok)
                if s + 1 < n:
                    go(f"{nm}{side}{s + 1}", dst, dst, dev, more)
                if nm == "x":
                    go(f"c{side}{s}", dst, dst, xn, ok)

    relay(1)
    got("z1", lambda: q0g.at[row, h, pd], rest)
    mine = lambda: q0g.at[row, h, pd]
    go("z1", mine, mine, up, rest & has_up)
    go("zx", mine, mine, xn, rest)
    w_q0()
    got("zx", lambda: q0g.at[row, oh, pd])
    go("zc", lambda: q0g.at[row, :, pd], lambda: q0g.at[row, :, pd], (mate, col))
    for d in range(1, nh):
        go(f"pi{d}", lambda: q0g.at[row, :, pd], lambda: q0g.at[row, :, pd],
           (lax.rem(hi + d, nh) * 2 + core, col))

    def far(d):
        return lax.rem(hi + nh - d, nh) * 2 + core

    def far_mate(d):
        return lax.rem(hi + nh - d, nh) * 2 + 1 - core

    def second(first_name, second_name, view):
        for d in range(1, nh):
            got(f"{first_name}{d}", lambda d=d: view(far(d)))
            go(f"{second_name}{d}", lambda d=d: view(far(d)), lambda d=d: view(far(d)), (mate, col))

    def all_in(near_name, second_name, view):
        got(near_name, lambda: view(mate))
        for d in range(1, nh):
            got(f"{second_name}{d}", lambda d=d: view(far_mate(d)))

    pv = lambda k: pg.at[k, :, pd]
    qv = lambda k: qg.at[k, pd]
    zv = lambda k: q0g.at[k, :, pd]
    second("ph", "pj", pv)
    second("pg", "pk", qv)
    for s in range(2, n):
        relay(s)
    second("pi", "pl", zv)
    all_in("p1", "pj", pv)
    w_y()

    t_at = lax.broadcasted_iota(jnp.int32, (hr, LANES), 0) + h * hr
    u_at = lax.broadcasted_iota(jnp.int32, (hr, LANES), 1)
    nt = (((1,), (1,)), ((), ()))
    tn = (((0,), (0,)), ((), ()))
    for k in range(n):
        value = sum(
            lax.dot_general(yg[k, :, i * width:(i + 1) * width], pg[k, i], nt, preferred_element_type=F32)
            for i in range(2)
        )
        live = (t_at < lr[row, k]) & (u_at < ur[k, zz])
        cb[k, pl.ds(h, 1)] = jnp.where(live, value, 0.0).astype(BF16)[None]
    go("cx", lambda: cb.at[:, h], lambda: cb.at[:, h], xn)
    got("cx", lambda: cb.at[:, oh])

    def keep():
        c0[...] = cb[...]
    on(first, keep)
    half = lambda: c0.at[:, h]
    go("c0", half, half, up, first)

    all_in("q1", "pk", qv)
    w_q()
    w_x()
    got("x0", lambda: xg.at[zz, oh])
    for s in range(1, n):
        got(f"cb{s}", lambda s=s: xg.at[lax.rem(zz - s + n, n), oh], zz - s >= 0)
        got(f"ca{s}", lambda s=s: xg.at[lax.rem(zz + s, n), oh], zz + s < n)
    w_tr()
    step = 256

    def update(at, _):
        rows = pl.ds(pl.multiple_of(at * step, step), step)
        for k in range(n):
            part = xg[k, :, :, rows].reshape(2 * hr, step)
            og[:, k * LANES:(k + 1) * LANES] = lax.dot_general(
                part, cb[k].reshape(2 * hr, LANES), tn, preferred_element_type=F32).astype(BF16)
        product = jnp.dot(og[...], qg[...].reshape(n * LANES, width), preferred_element_type=F32)
        ub[rows, :] = (tr[rows, :].astype(F32) - product).astype(BF16)
        return 0

    lax.fori_loop(0, tile // step, update, 0)
    w_up = local(7, ref(ub), ref(up_out))

    got("fw1", ref(pf), rest)
    go("pfx", ref(pf), lambda: pin.at[h], xn, rest)
    got("c0", half, rest)
    go("c0", half, half, up, rest & has_up)
    go("c0x", half, half, xn, rest)
    got("c0x", lambda: c0.at[:, oh], rest)
    all_in("zc", "pl", zv)
    blk = og0.shape[0]
    lanes = pl.ds(pl.multiple_of(col * sr // blk * blk, blk), blk)
    inside = pl.ds(pl.multiple_of(lax.rem(col * sr, blk), sr), sr)
    for k in range(n):
        part = xg[k, :, :, lanes].reshape(2 * hr, blk)
        og0[:, k * LANES:(k + 1) * LANES] = lax.dot_general(
            part, c0[k].reshape(2 * hr, LANES), tn, preferred_element_type=F32).astype(BF16)
    for i in range(2):
        prod0[i] = jnp.dot(og0[...], q0g[:, i].reshape(n * LANES, width), preferred_element_type=F32)
    got("pfx", lambda: pin.at[oh])
    w_pin()
    got("ow1", lambda: pin.at[h], rest)
    for i in range(2):
        nb[:, i * width:(i + 1) * width] = (pin[i].astype(F32) - prod0[i, inside, :]).astype(BF16)
    w_np = local(8, ref(nb), ref(np_out))
    for cond, f in pending:
        on(cond, f)
    w_up()
    w_np()


def body(trailing, left_outer, left_inner, upper_outer, upper_inner, left_ranks, upper_ranks):
    n = lax.axis_size("row")
    nc = lax.axis_size("col")
    tile, width = trailing.shape
    hr = left_outer.shape[0]
    sr = tile // nc
    blk = max(sr, LANES)
    names = sem_names(n, n // 2)
    any_space = pl.BlockSpec(memory_space=pl.ANY)
    smem = pl.BlockSpec(memory_space=pltpu.SMEM)
    vmem = pltpu.VMEM
    return pl.pallas_call(
        functools.partial(kernel, n, names),
        out_shape=(
            jax.ShapeDtypeStruct((tile, width), BF16),
            jax.ShapeDtypeStruct((sr, 2 * width), BF16),
        ),
        in_specs=[any_space] * 5 + [smem] * 2,
        out_specs=(any_space, any_space),
        scratch_shapes=[
            vmem((n, 2, hr, tile), BF16),
            vmem((n, hr, tile), BF16),
            vmem((n, 2, LANES, width), BF16),
            vmem((n, LANES, width), BF16),
            vmem((n, 2, LANES, width), BF16),
            vmem((n, 2, hr, LANES), BF16),
            vmem((n, 2, hr, LANES), BF16),
            vmem((256, n * LANES), BF16),
            vmem((blk, n * LANES), BF16),
            vmem((2, blk, width), F32),
            vmem((tile, width), BF16),
            vmem((tile, width), BF16),
            vmem((sr, width), BF16),
            vmem((2, sr, width), BF16),
            vmem((sr, 2 * width), BF16),
            pltpu.SemaphoreType.DMA((len(names),)),
            pltpu.SemaphoreType.DMA((len(names),)),
            pltpu.SemaphoreType.DMA((9,)),
        ],
        compiler_params=pltpu.CompilerParams(
            collective_id=0, has_side_effects=True, vmem_limit_bytes=44 * 2 ** 20
        ),
        cost_estimate=pl.CostEstimate(
            flops=2 * tile * width * n * LANES, bytes_accessed=4 * tile * width, transcendentals=0
        ),
    )(trailing, left_outer, left_inner, upper_outer, upper_inner, left_ranks, upper_ranks)


def solution(mesh):
    in_specs = (
        P("row", "col"),
        P("col", "row"),
        P("col", "row"),
        P("row", "col"),
        P("row", "col"),
        P(),
        P(),
    )
    out_specs = (P("row", "col"), P(("row", "col"), None))
    return jax.shard_map(body, mesh=mesh, in_specs=in_specs, out_specs=out_specs, check_vma=False)
```

time: 205 us -> 58.2 us (0.28); the launches traced: 201 us -> 57.9 us
  waiting for transfers between devices: 131 us -> 0 us
  Pallas kernels: 0 us -> 49.4 us
  starting transfers between devices: 18.8 us -> 0 us
  blocking collectives: 15.4 us -> 0 us
  between operations: 14.1 us -> 0.66 us
  other arithmetic: 8.16 us -> 0 us
  matrix products: 7.77 us -> 0 us
    psum x1 -> x0, waiting for transfers between devices: 106 us -> none  [from_root(): return lax.psum(block, axis)]
    pallas_call x0 -> x1, Pallas kernels: none -> 49.4 us  [body(): pl.pallas_call(functools.partial(kernel, n, names), out_shape=(jax.ShapeD...]
    ppermute x8 -> x0, waiting for transfers between devices: 24.1 us -> none  [the longest x7 24.1 us: passed_along(): return lax.ppermute(value, axis, pairs)]
    ppermute x8 -> x0, starting transfers between devices: 18.8 us -> none  [the longest x7 17.2 us: passed_along(): return lax.ppermute(value, axis, pairs)]
    all_gather x2 -> x0, blocking collectives: 15.4 us -> none  [the longest x1 8.72 us: body(): lax.all_gather(top_rows, 'row', axis=0, tiled=True)]
    unnamed x2 -> x16, local copies, waits for them, and re-layouts: 0.01 us -> 7.82 us
    dot_general x9 -> x0, matrix products: 7.77 us -> none  [the longest x8 3.98 us: contribute(): lax.dot_general(outer_rows, central_block, (((0,), (0,)), ((), ())), pref...]
    dynamic_slice x9 -> x0, local copies, waits for them, and re-layouts: 5.47 us -> none  [the longest x8 5.29 us: contribute(): rank_here = lax.dynamic_index_in_dim(row_ranks, panel_at, 0, keepdims=False)]
  transfers between devices with their start and end apart: 9 -> 0, of which waited for: 8 -> 0; matrix products, arithmetic and copies ran while one was open for 8% -> 0% of each run, Pallas kernels for 0% -> 0%
where the time goes in v1:
time: 58.2 us; the launch traced here: 57.9 us
  Pallas kernels  49.4 us (85%)
  local copies, waits for them, and re-layouts  7.82 us (13%)
  between operations  0.66 us (1%)
    pallas_call x1, Pallas kernels, body(): pl.pallas_call(functools.partial(kernel, n, names), out_shape=(jax.ShapeD...  49.4 us
    unnamed x16, local copies, waits for them, and re-layouts  7.82 us

profile of v1, /device:TPU:24, one launch (start us, length us, event | category | flops | bytes accessed | tf_op | source)
XLA Modules:
  0.0 57.9 jit_solution(9203093853395681273)
XLA Ops:
  0.6 0.0 copy-start
  0.6 1.2 %copy-done = bf16[1024,512]{1,0:T(8,128)(2,1)S(1)} copy-done((bf16[1024,512]{1,0:T(8,128)(2,1)S(1)}, bf16[1024,512]{1,0:T(8,128)(2,1)}, u32[]{:S(2)}) %copy-start) | copy-done | bytes 1048600
  1.9 0.0 copy-start.1
  1.9 0.9 %copy-done.1 = bf16[48,1024]{1,0:T(8,128)(2,1)S(1)} copy-done((bf16[48,1024]{1,0:T(8,128)(2,1)S(1)}, bf16[48,1024]{1,0:T(8,128)(2,1)}, u32[]{:S(2)}) %copy-start.1) | copy-done | bytes 98328
  2.8 0.0 copy-start.2
  2.8 0.9 %copy-done.2 = bf16[48,1024]{1,0:T(8,128)(2,1)S(1)} copy-done((bf16[48,1024]{1,0:T(8,128)(2,1)S(1)}, bf16[48,1024]{1,0:T(8,128)(2,1)}, u32[]{:S(2)}) %copy-start.2) | copy-done | bytes 98328
  3.6 0.0 copy-start.3
  3.6 0.9 %copy-done.3 = bf16[96,512]{1,0:T(8,128)(2,1)S(1)} copy-done((bf16[96,512]{1,0:T(8,128)(2,1)S(1)}, bf16[96,512]{1,0:T(8,128)(2,1)}, u32[]{:S(2)}) %copy-start.3) | copy-done | bytes 98328
  4.5 0.0 copy-start.4
  4.5 0.9 %copy-done.4 = bf16[96,512]{1,0:T(8,128)(2,1)S(1)} copy-done((bf16[96,512]{1,0:T(8,128)(2,1)S(1)}, bf16[96,512]{1,0:T(8,128)(2,1)}, u32[]{:S(2)}) %copy-start.4) | copy-done | bytes 98328
  5.4 0.0 copy-start.5
  5.4 0.7 %copy-done.5 = s32[4,4]{1,0:T(4,128)S(1)} copy-done((s32[4,4]{1,0:T(4,128)S(1)}, s32[4,4]{1,0:T(4,128)}, u32[]{:S(2)}) %copy-start.5) | copy-done | bytes 88
  6.1 0.0 copy-start.6
  6.1 0.7 %copy-done.6 = s32[4,4]{1,0:T(4,128)S(1)} copy-done((s32[4,4]{1,0:T(4,128)S(1)}, s32[4,4]{1,0:T(4,128)}, u32[]{:S(2)}) %copy-start.6) | copy-done | bytes 88
  6.8 49.4 %shard_map.86 = (bf16[1024,512]{1,0:T(8,128)(2,1)S(1)}, bf16[128,1024]{1,0:T(8,128)(2,1)S(1)}) custom-call(bf16[1024,512]{1,0:T(8,128)(2,1)S(1)} %copy-done, bf16[48,1024]{1,0:T(8,128)(2,1)S(1)} %copy-done.1, bf16[48,1024]{1,0:T(8,128)(2,1)S(1)} %copy-done.2, bf16[96,512]{1,0:T(8,128)(2,1)S(1)} %copy-done.3, bf16[96,512]{1,0:T(8,128)(2,1)S(1)} %copy-done.4, ...), custom_call_target="tpu_custom_call" | custom-call | flops 536870912 | bytes 2097152 | tf_op jit(solution)/shard_map/pallas_call | solution.py:262
  56.2 1.0 %copy.11 = bf16[1024,512]{1,0:T(8,128)(2,1)} copy(bf16[1024,512]{1,0:T(8,128)(2,1)S(1)} %get-tuple-element.4) | data formatting | bytes 2097152
  57.2 0.7 %copy.12 = bf16[128,1024]{1,0:T(8,128)(2,1)} copy(bf16[128,1024]{1,0:T(8,128)(2,1)S(1)} %get-tuple-element.5) | data formatting | bytes 524288
Async XLA Ops:
  0.6 1.2 %copy-start = (bf16[1024,512]{1,0:T(8,128)(2,1)S(1)}, bf16[1024,512]{1,0:T(8,128)(2,1)}, u32[]{:S(2)}) copy-start(bf16[1024,512]{1,0:T(8,128)(2,1)} %tr_in.1) | copy-start | bytes 3145732
  1.9 0.9 %copy-start.1 = (bf16[48,1024]{1,0:T(8,128)(2,1)S(1)}, bf16[48,1024]{1,0:T(8,128)(2,1)}, u32[]{:S(2)}) copy-start(bf16[48,1024]{1,0:T(8,128)(2,1)} %x_in.1) | copy-start | bytes 294916
  2.8 0.9 %copy-start.2 = (bf16[48,1024]{1,0:T(8,128)(2,1)S(1)}, bf16[48,1024]{1,0:T(8,128)(2,1)}, u32[]{:S(2)}) copy-start(bf16[48,1024]{1,0:T(8,128)(2,1)} %y_in.1) | copy-start | bytes 294916
  3.6 0.9 %copy-start.3 = (bf16[96,512]{1,0:T(8,128)(2,1)S(1)}, bf16[96,512]{1,0:T(8,128)(2,1)}, u32[]{:S(2)}) copy-start(bf16[96,512]{1,0:T(8,128)(2,1)} %p_in.1) | copy-start | bytes 294916
  4.5 0.9 %copy-start.4 = (bf16[96,512]{1,0:T(8,128)(2,1)S(1)}, bf16[96,512]{1,0:T(8,128)(2,1)}, u32[]{:S(2)}) copy-start(bf16[96,512]{1,0:T(8,128)(2,1)} %q_in.1) | copy-start | bytes 294916
  5.4 0.7 %copy-start.5 = (s32[4,4]{1,0:T(4,128)S(1)}, s32[4,4]{1,0:T(4,128)}, u32[]{:S(2)}) copy-start(s32[4,4]{1,0:T(4,128)} %lr.1) | copy-start | bytes 196
  6.1 0.7 %copy-start.6 = (s32[4,4]{1,0:T(4,128)S(1)}, s32[4,4]{1,0:T(4,128)}, u32[]{:S(2)}) copy-start(s32[4,4]{1,0:T(4,128)} %ur.1) | copy-start | bytes 196

commit v2 on v1

--- a/solution.py
+++ b/solution.py
@@ -107,10 +107,11 @@
         return pl.ds(pl.multiple_of((z * 2 + side) * sr, sr), sr)
 
     go("pfx", lambda: tr_in.at[rows_of(0, oh)], lambda: pin.at[h], xn, first)
-    for s in range(n - 1, 0, -1):
-        go(f"fw{s}", lambda s=s: tr_in.at[rows_of(s, oh)], ref(pf), (row, s * 2 + h), first, "fw1")
-    for s in range(n - 1, 0, -1):
-        go(f"ow{s}", lambda s=s: tr_in.at[rows_of(s, h)], lambda: pin.at[h], (row, s * 2 + h), first, "ow1")
+
+    def feed(s):
+        go(f"fw{s}", lambda: tr_in.at[rows_of(s, oh)], ref(pf), (row, s * 2 + h), first, "fw1")
+        go(f"ow{s}", lambda: tr_in.at[rows_of(s, h)], lambda: pin.at[h], (row, s * 2 + h), first, "ow1")
+
     w_pin = local(5, lambda: tr_in.at[rows_of(0, h)], lambda: pin.at[h], first)
     w_tr = local(6, ref(tr_in), ref(tr))
 
@@ -139,6 +140,7 @@
                     go(f"c{side}{s}", dst, dst, xn, ok)
 
     relay(1)
+    feed(1)
     got("z1", lambda: q0g.at[row, h, pd], rest)
     mine = lambda: q0g.at[row, h, pd]
     go("z1", mine, mine, up, rest & has_up)
@@ -173,6 +175,7 @@
     second("pg", "pk", qv)
     for s in range(2, n):
         relay(s)
+        feed(s)
     second("pi", "pl", zv)
     all_in("p1", "pj", pv)
     w_y()
@@ -288,7 +291,7 @@
             pltpu.SemaphoreType.DMA((9,)),
         ],
         compiler_params=pltpu.CompilerParams(
-            collective_id=0, has_side_effects=True, vmem_limit_bytes=44 * 2 ** 20
+            collective_id=0, has_side_effects=True, vmem_limit_bytes=60 * 2 ** 20
         ),
         cost_estimate=pl.CostEstimate(
             flops=2 * tile * width * n * LANES, bytes_accessed=4 * tile * width, transcendentals=0

time: 58.2 us -> 47.4 us (0.81)
  Pallas kernels: 49.4 us -> 43.6 us
  local copies, waits for them, and re-layouts: 7.82 us -> 3.01 us
    pallas_call x1, Pallas kernels: 49.4 us -> 43.6 us  [body(): pl.pallas_call(functools.partial(kernel, n, names), out_shape=(jax.ShapeD...]
    unnamed x16 -> x4, local copies, waits for them, and re-layouts: 7.82 us -> 3.01 us
where the time goes in v2:
time: 47.4 us; the launch traced here: 47.2 us
  Pallas kernels  43.6 us (92%)
  local copies, waits for them, and re-layouts  3.01 us (6%)
  between operations  0.65 us (1%)
    pallas_call x1, Pallas kernels, body(): pl.pallas_call(functools.partial(kernel, n, names), out_shape=(jax.ShapeD...  43.6 us
    unnamed x4, local copies, waits for them, and re-layouts  3.01 us

profile of v2, /device:TPU:24, one launch (start us, length us, event | category | flops | bytes accessed | tf_op | source)
XLA Modules:
  0.0 47.2 jit_solution(15438319887632640586)
XLA Ops:
  0.6 43.6 %shard_map.86 = (bf16[1024,512]{1,0:T(8,128)(2,1)}, bf16[128,1024]{1,0:T(8,128)(2,1)}) custom-call(bf16[1024,512]{1,0:T(8,128)(2,1)} %tr_in.1, bf16[48,1024]{1,0:T(8,128)(2,1)} %x_in.1, bf16[48,1024]{1,0:T(8,128)(2,1)} %y_in.1, bf16[96,512]{1,0:T(8,128)(2,1)} %p_in.1, bf16[96,512]{1,0:T(8,128)(2,1)} %q_in.1, s32[4,4]{1,0:T(4,128)} %lr.1, s32[4,4]{1,0:T(4,128)} %ur.1), custom_call_target="tpu_custom_call" | custom-call | flops 536870912 | bytes 2097152 | tf_op jit(solution)/shard_map/pallas_call | solution.py:265
  44.2 0.0 copy-start
  44.2 2.3 %copy.11 = bf16[1024,512]{1,0:T(8,128)(2,1)} copy(bf16[1024,512]{1,0:T(8,128)(2,1)} %get-tuple-element.4) | data formatting | bytes 2097152
  46.5 0.0 copy-done
  46.5 0.7 %copy.12 = bf16[128,1024]{1,0:T(8,128)(2,1)} copy(bf16[128,1024]{1,0:T(8,128)(2,1)S(1)} %copy-done) | data formatting | bytes 524288
Async XLA Ops:
  44.2 2.3 %copy-start = (bf16[128,1024]{1,0:T(8,128)(2,1)S(1)}, bf16[128,1024]{1,0:T(8,128)(2,1)}, u32[]{:S(2)}) copy-start(bf16[128,1024]{1,0:T(8,128)(2,1)} %get-tuple-element.5) | copy-start | bytes 786436

commit v3 on v2

--- a/solution.py
+++ b/solution.py
@@ -62,7 +62,12 @@
                 src_ref=src(), dst_ref=dst(), send_sem=ssem.at[names[name]],
                 recv_sem=rsem.at[at], device_id=dev, device_id_type=MESH)
         on(cond, lambda: make().start())
-        pending.append((cond, lambda: make().wait_send()))
+        pending.append((name, cond, lambda: make().wait_send()))
+
+    def sent(name):
+        for entry in [e for e in pending if e[0] == name]:
+            on(*entry[1:])
+            pending.remove(entry)
 
     def got(name, dst, cond=None):
         on(cond, lambda: desc(name, dst, dst, xn).wait_recv())
@@ -91,9 +96,6 @@
         go(nm + "b1", ref(src), lambda dst=dst: dst(zz), up, has_up)
         go(nm + "a1", ref(src), lambda dst=dst: dst(zz), down, has_down)
     go("px", ref(p_in), lambda: pg.at[row, h, pd], xn)
-    go("x0", ref(x_in), lambda: xg.at[zz, h], xn)
-    go("z1", ref(q_in), lambda: q0g.at[row, h, pd], up, first)
-    go("zx", ref(q_in), lambda: q0g.at[row, h, pd], xn, first)
     go("q1", ref(q_in), lambda: qg.at[row, pd], (mate, col))
     for d in range(1, nh):
         go(f"pg{d}", ref(q_in), lambda: qg.at[row, pd], (lax.rem(hi + d, nh) * 2 + core, col))
@@ -108,8 +110,10 @@
 
     go("pfx", lambda: tr_in.at[rows_of(0, oh)], lambda: pin.at[h], xn, first)
 
-    def feed(s):
+    def across(s):
         go(f"fw{s}", lambda: tr_in.at[rows_of(s, oh)], ref(pf), (row, s * 2 + h), first, "fw1")
+
+    def along(s):
         go(f"ow{s}", lambda: tr_in.at[rows_of(s, h)], lambda: pin.at[h], (row, s * 2 + h), first, "ow1")
 
     w_pin = local(5, lambda: tr_in.at[rows_of(0, h)], lambda: pin.at[h], first)
@@ -122,6 +126,8 @@
 
     w_p()
     got("px", lambda: pg.at[row, oh, pd])
+    go("x0", ref(x_in), lambda: xg.at[zz, h], xn)
+    go("zx", ref(q_in), lambda: q0g.at[row, h, pd], xn, first)
     go("p1", lambda: pg.at[row, :, pd], lambda: pg.at[row, :, pd], (mate, col))
     for d in range(1, nh):
         go(f"ph{d}", lambda: pg.at[row, :, pd], lambda: pg.at[row, :, pd],
@@ -139,19 +145,6 @@
                 if nm == "x":
                     go(f"c{side}{s}", dst, dst, xn, ok)
 
-    relay(1)
-    feed(1)
-    got("z1", lambda: q0g.at[row, h, pd], rest)
-    mine = lambda: q0g.at[row, h, pd]
-    go("z1", mine, mine, up, rest & has_up)
-    go("zx", mine, mine, xn, rest)
-    w_q0()
-    got("zx", lambda: q0g.at[row, oh, pd])
-    go("zc", lambda: q0g.at[row, :, pd], lambda: q0g.at[row, :, pd], (mate, col))
-    for d in range(1, nh):
-        go(f"pi{d}", lambda: q0g.at[row, :, pd], lambda: q0g.at[row, :, pd],
-           (lax.rem(hi + d, nh) * 2 + core, col))
-
     def far(d):
         return lax.rem(hi + nh - d, nh) * 2 + core
 
@@ -171,12 +164,27 @@
     pv = lambda k: pg.at[k, :, pd]
     qv = lambda k: qg.at[k, pd]
     zv = lambda k: q0g.at[k, :, pd]
-    second("ph", "pj", pv)
+    mine = lambda: q0g.at[row, h, pd]
+    relay(1)
+    go("z1", ref(q_in), mine, up, first)
+    across(1)
     second("pg", "pk", qv)
     for s in range(2, n):
         relay(s)
-        feed(s)
-    second("pi", "pl", zv)
+        if s == 2:
+            second("ph", "pj", pv)
+        if s < n - 1:
+            along(s - 1)
+        across(s)
+
+    def first_column(cond, more):
+        got("z1", mine, cond)
+        if more:
+            go("z1", mine, mine, up, cond)
+        go("zx", mine, mine, xn, cond)
+
+    middle, last = rest & has_up, zz == n - 1
+    first_column(middle, True)
     all_in("p1", "pj", pv)
     w_y()
 
@@ -192,6 +200,10 @@
         live = (t_at < lr[row, k]) & (u_at < ur[k, zz])
         cb[k, pl.ds(h, 1)] = jnp.where(live, value, 0.0).astype(BF16)[None]
     go("cx", lambda: cb.at[:, h], lambda: cb.at[:, h], xn)
+    first_column(last, False)
+    sent("fw1")
+    sent(f"fw{n - 2}")
+    along(n - 2)
     got("cx", lambda: cb.at[:, oh])
 
     def keep():
@@ -199,6 +211,22 @@
     on(first, keep)
     half = lambda: c0.at[:, h]
     go("c0", half, half, up, first)
+    w_q0()
+    got("zx", lambda: q0g.at[row, oh, pd])
+    go("zc", lambda: q0g.at[row, :, pd], lambda: q0g.at[row, :, pd], (mate, col))
+    for d in range(1, nh):
+        go(f"pi{d}", lambda: q0g.at[row, :, pd], lambda: q0g.at[row, :, pd],
+           (lax.rem(hi + d, nh) * 2 + core, col))
+
+    def relay_first(cond, more):
+        got("fw1", ref(pf), cond)
+        go("pfx", ref(pf), lambda: pin.at[h], xn, cond)
+        got("c0", half, cond)
+        if more:
+            go("c0", half, half, up, cond)
+        go("c0x", half, half, xn, cond)
+
+    relay_first(middle, True)
 
     all_in("q1", "pk", qv)
     w_q()
@@ -223,11 +251,10 @@
     lax.fori_loop(0, tile // step, update, 0)
     w_up = local(7, ref(ub), ref(up_out))
 
-    got("fw1", ref(pf), rest)
-    go("pfx", ref(pf), lambda: pin.at[h], xn, rest)
-    got("c0", half, rest)
-    go("c0", half, half, up, rest & has_up)
-    go("c0x", half, half, xn, rest)
+    sent(f"fw{n - 1}")
+    along(n - 1)
+    second("pi", "pl", zv)
+    relay_first(last, False)
     got("c0x", lambda: c0.at[:, oh], rest)
     all_in("zc", "pl", zv)
     blk = og0.shape[0]
@@ -245,8 +272,8 @@
     for i in range(2):
         nb[:, i * width:(i + 1) * width] = (pin[i].astype(F32) - prod0[i, inside, :]).astype(BF16)
     w_np = local(8, ref(nb), ref(np_out))
-    for cond, f in pending:
-        on(cond, f)
+    for entry in pending:
+        on(*entry[1:])
     w_up()
     w_np()
 
@@ -291,7 +318,7 @@
             pltpu.SemaphoreType.DMA((9,)),
         ],
         compiler_params=pltpu.CompilerParams(
-            collective_id=0, has_side_effects=True, vmem_limit_bytes=60 * 2 ** 20
+            collective_id=0, has_side_effects=True, vmem_limit_bytes=56 * 2 ** 20
         ),
         cost_estimate=pl.CostEstimate(
             flops=2 * tile * width * n * LANES, bytes_accessed=4 * tile * width, transcendentals=0

time: 47.4 us -> 44.5 us (0.939)
  Pallas kernels: 43.6 us -> 40.7 us
    pallas_call x1, Pallas kernels: 43.6 us -> 40.7 us  [body(): pl.pallas_call(functools.partial(kernel, n, names), out_shape=(jax.ShapeD...]
where the time goes in v3:
time: 44.5 us; the launch traced here: 44.3 us
  Pallas kernels  40.7 us (91%)
  local copies, waits for them, and re-layouts  3.01 us (7%)
  between operations  0.65 us (1%)
    pallas_call x1, Pallas kernels, body(): pl.pallas_call(functools.partial(kernel, n, names), out_shape=(jax.ShapeD...  40.7 us
    unnamed x4, local copies, waits for them, and re-layouts  3.01 us

profile of v3, /device:TPU:24, one launch (start us, length us, event | category | flops | bytes accessed | tf_op | source)
XLA Modules:
  0.0 44.3 jit_solution(1125804786745050008)
XLA Ops:
  0.6 40.7 %shard_map.86 = (bf16[1024,512]{1,0:T(8,128)(2,1)}, bf16[128,1024]{1,0:T(8,128)(2,1)}) custom-call(bf16[1024,512]{1,0:T(8,128)(2,1)} %tr_in.1, bf16[48,1024]{1,0:T(8,128)(2,1)} %x_in.1, bf16[48,1024]{1,0:T(8,128)(2,1)} %y_in.1, bf16[96,512]{1,0:T(8,128)(2,1)} %p_in.1, bf16[96,512]{1,0:T(8,128)(2,1)} %q_in.1, s32[4,4]{1,0:T(4,128)} %lr.1, s32[4,4]{1,0:T(4,128)} %ur.1), custom_call_target="tpu_custom_call" | custom-call | flops 536870912 | bytes 2097152 | tf_op jit(solution)/shard_map/pallas_call | solution.py:292
  41.3 0.0 copy-start
  41.3 2.3 %copy.11 = bf16[1024,512]{1,0:T(8,128)(2,1)} copy(bf16[1024,512]{1,0:T(8,128)(2,1)} %get-tuple-element.4) | data formatting | bytes 2097152
  43.6 0.0 copy-done
  43.6 0.7 %copy.12 = bf16[128,1024]{1,0:T(8,128)(2,1)} copy(bf16[128,1024]{1,0:T(8,128)(2,1)S(1)} %copy-done) | data formatting | bytes 524288
Async XLA Ops:
  41.3 2.3 %copy-start = (bf16[128,1024]{1,0:T(8,128)(2,1)S(1)}, bf16[128,1024]{1,0:T(8,128)(2,1)}, u32[]{:S(2)}) copy-start(bf16[128,1024]{1,0:T(8,128)(2,1)} %get-tuple-element.5) | copy-start | bytes 786436

commit v4 on v3

v4 whole, which is shorter than its diff:
```python
import functools

import jax
import jax.numpy as jnp
from jax import lax
from jax.experimental import pallas as pl
from jax.experimental.pallas import tpu as pltpu
from jax.sharding import PartitionSpec as P

MESH = pl.DeviceIdType.MESH
LANES = 128
F32 = jnp.float32
BF16 = jnp.bfloat16


def sem_names(n, nh):
    names = ["px", "x0", "q1", "p1", "q1p", "z1", "zc", "cx", "c0", "c0x", "pfx"]
    for s in range(1, n):
        names += [f"xb{s}", f"xa{s}", f"yb{s}", f"ya{s}", f"cb{s}", f"ca{s}"]
        names += [f"fw{s}", f"ow{s}"]
    for d in range(1, nh):
        names += [f"p{a}{d}" for a in "ghijklmn"]
    return {name: at for at, name in enumerate(names)}


def kernel(n, names, tr_in, x_in, y_in, p_in, q_in, lr, ur, up_out, np_out,
           xg, yg, pg, qg, q0g, cb, c0, og, og0, prod0, tr, ub, raw, nb,
           ssem, rsem, lsem):
    nh = n // 2
    rank = p_in.shape[0]
    hr = x_in.shape[0]
    tile, width = tr_in.shape
    sr = np_out.shape[0]
    row, col = lax.axis_index("row"), lax.axis_index("col")
    zz, h = col // 2, col % 2
    oh = 1 - h
    hi, core = row // 2, row % 2
    mate = hi * 2 + (1 - core)
    xn = (row, zz * 2 + oh)
    up = (row, lax.rem(zz + 1, n) * 2 + h)
    down = (row, lax.rem(zz + n - 1, n) * 2 + h)
    first, rest = zz == 0, zz > 0
    has_up, has_down = zz < n - 1, zz > 0
    pending = []

    def on(cond, f):
        if cond is None:
            f()
        else:
            pl.when(cond)(f)

    def desc(name, src, dst, dev):
        at = names[name]
        return pltpu.make_async_remote_copy(
            src_ref=src(), dst_ref=dst(), send_sem=ssem.at[at], recv_sem=rsem.at[at],
            device_id=dev, device_id_type=MESH)

    def go(name, src, dst, dev, cond=None, sem=None):
        def make():
            at = names[sem or name]
            return pltpu.make_async_remote_copy(
                src_ref=src(), dst_ref=dst(), send_sem=ssem.at[names[name]],
                recv_sem=rsem.at[at], device_id=dev, device_id_type=MESH)
        on(cond, lambda: make().start())
        pending.append((name, cond, lambda: make().wait_send()))

    def sent(name):
        for entry in [e for e in pending if e[0] == name]:
            on(*entry[1:])
            pending.remove(entry)

    def got(name, dst, cond=None):
        on(cond, lambda: desc(name, dst, dst, xn).wait_recv())

    def local(at, src, dst, cond=None):
        def make():
            return pltpu.make_async_copy(src(), dst(), lsem.at[at])
        on(cond, lambda: make().start())
        return lambda: on(cond, lambda: make().wait())

    partners = [xn, (mate, col)]
    for s in range(1, n):
        partners.append((row, lax.rem(zz + s, n) * 2 + h))
    for d in range(1, nh):
        partners.append((lax.rem(hi + d, nh) * 2 + core, col))
    barrier = pltpu.get_barrier_semaphore()
    for dev in partners:
        pl.semaphore_signal(barrier, inc=1, device_id=dev, device_id_type=MESH)
    pl.semaphore_wait(barrier, len(partners))

    def ref(r):
        return lambda: r

    pd = pl.ds(0, rank)
    fars = [(d, (lax.rem(hi + d, nh) * 2 + core, col)) for d in range(1, nh)]
    near = (mate, col)
    middle, last = rest & has_up, zz == n - 1
    yv, xv = (lambda k: yg.at[k]), (lambda k: xg.at[k, h])
    pv = lambda side: lambda k: pg.at[k, side, pd]
    qv, zv = (lambda k: qg.at[k, pd]), (lambda k: q0g.at[k, pd])

    def spread(near_name, far_name, view, src=None):
        src = src or (lambda: view(row))
        go(near_name, src, lambda: view(row), near)
        for d, dev in fars:
            go(f"{far_name}{d}", src, lambda: view(row), dev)

    def far(d):
        return lax.rem(hi + nh - d, nh) * 2 + core

    def far_mate(d):
        return lax.rem(hi + nh - d, nh) * 2 + 1 - core

    def second(first_name, second_name, view, cond=None):
        for d in range(1, nh):
            got(f"{first_name}{d}", lambda d=d: view(far(d)), cond)
            go(f"{second_name}{d}", lambda d=d: view(far(d)), lambda d=d: view(far(d)), near, cond)

    def all_in(near_name, second_name, view, cond=None):
        got(near_name, lambda: view(mate), cond)
        for d in range(1, nh):
            got(f"{second_name}{d}", lambda d=d: view(far_mate(d)), cond)

    go("yb1", ref(y_in), lambda: yv(zz), up, has_up)
    go("ya1", ref(y_in), lambda: yv(zz), down, has_down)
    go("px", ref(p_in), lambda: pv(h)(row), xn)
    spread("p1", "pg", pv(h), ref(p_in))
    w_p = local(0, ref(p_in), lambda: pv(h)(row))
    w_x = local(1, ref(x_in), lambda: xv(zz))
    w_y = local(2, ref(y_in), lambda: yv(zz))
    w_q = local(3, ref(q_in), lambda: qv(row))

    def rows_of(z, side):
        return pl.ds(pl.multiple_of((z * 2 + side) * sr, sr), sr)

    def across(s):
        go(f"fw{s}", lambda: tr_in.at[rows_of(s, oh)], lambda: raw.at[oh], (row, s * 2 + h), first, "fw1")

    def along(s):
        go(f"ow{s}", lambda: tr_in.at[rows_of(s, h)], lambda: raw.at[h], (row, s * 2 + h), first, "ow1")

    w_raw = [local(5 + i, lambda i=i: tr_in.at[rows_of(0, i)], lambda i=i: raw.at[i], first) for i in range(2)]
    w_tr = local(7, ref(tr_in), ref(tr))

    pad = LANES - rank
    pg[:, :, rank:, :] = jnp.zeros((n, 2, pad, width), BF16)
    qg[:, rank:, :] = jnp.zeros((n, pad, width), BF16)

    def pad_first():
        q0g[:, rank:, :] = jnp.zeros((n, pad, width), BF16)
    on(rest, pad_first)

    got("px", lambda: pv(oh)(row))
    spread("q1p", "ph", pv(oh))

    def relay(nm, s, view):
        for side, dev, ok, more, slot in (
            ("b", up, zz - s >= 0, (zz - s >= 0) & has_up, lax.rem(zz - s + n, n)),
            ("a", down, zz + s < n, (zz + s < n) & has_down, lax.rem(zz + s, n)),
        ):
            dst = lambda slot=slot: view(slot)
            got(f"{nm}{side}{s}", dst, ok)
            if s + 1 < n:
                go(f"{nm}{side}{s + 1}", dst, dst, dev, more)
            if nm == "x":
                go(f"c{side}{s}", dst, dst, xn, ok)

    relay("y", 1, yv)
    go("xb1", ref(x_in), lambda: xv(zz), up, first)
    across(1)
    second("pg", "pi", pv(h))
    for s in range(2, n):
        relay("y", s, yv)
        if s == 2:
            go("xb1", ref(x_in), lambda: xv(zz), up, middle)
            go("xa1", ref(x_in), lambda: xv(zz), down, has_down)
            go("x0", ref(x_in), lambda: xv(zz), xn)
            go("z1", ref(q_in), lambda: zv(row), up, first)
            along(1)
            second("ph", "pj", pv(oh))
    spread("q1", "pk", qv, ref(q_in))
    w_p()
    w_y()
    all_in("p1", "pi", pv(h))
    all_in("q1p", "pj", pv(oh))

    t_at = lax.broadcasted_iota(jnp.int32, (hr, LANES), 0) + h * hr
    u_at = lax.broadcasted_iota(jnp.int32, (hr, LANES), 1)
    nt = (((1,), (1,)), ((), ()))
    tn = (((0,), (0,)), ((), ()))
    for k in range(n):
        value = sum(
            lax.dot_general(yg[k, :, i * width:(i + 1) * width], pg[k, i], nt, preferred_element_type=F32)
            for i in range(2)
        )
        live = (t_at < lr[row, k]) & (u_at < ur[k, zz])
        cb[k, pl.ds(h, 1)] = jnp.where(live, value, 0.0).astype(BF16)[None]
    go("cx", lambda: cb.at[:, h], lambda: cb.at[:, h], xn)
    relay("x", 1, xv)
    got("cx", lambda: cb.at[:, oh])

    def keep():
        c0[...] = cb[...]
    on(first, keep)
    half = lambda: c0.at[:, h]
    go("c0", half, half, up, first)
    if n > 2:
        across(2)

    def first_column(cond, more):
        got("z1", lambda: zv(row), cond)
        if more:
            go("z1", lambda: zv(row), lambda: zv(row), up, cond)
        go("zc", lambda: zv(row), lambda: zv(row), near, cond)
        for d, dev in fars:
            go(f"pl{d}", lambda: zv(row), lambda: zv(row), dev, cond)

    def relay_core(cond, more):
        got("c0", half, cond)
        if more:
            go("c0", half, half, up, cond)
        go("c0x", half, half, xn, cond)

    first_column(middle, True)
    relay("x", 2, xv)
    relay_core(middle, True)
    for s in range(3, n):
        relay("x", s, xv)
        across(s)
    first_column(last, False)
    second("pk", "pm", qv)
    for s in range(2, n - 1):
        sent(f"fw{s}")
        along(s)
    relay_core(last, False)

    all_in("q1", "pm", qv)
    w_q()
    w_x()
    got("x0", lambda: xg.at[zz, oh])
    for s in range(1, n):
        got(f"cb{s}", lambda s=s: xg.at[lax.rem(zz - s + n, n), oh], zz - s >= 0)
        got(f"ca{s}", lambda s=s: xg.at[lax.rem(zz + s, n), oh], zz + s < n)
    w_tr()
    step = 256

    def update(at, _):
        rows = pl.ds(pl.multiple_of(at * step, step), step)
        for k in range(n):
            part = xg[k, :, :, rows].reshape(2 * hr, step)
            og[:, k * LANES:(k + 1) * LANES] = lax.dot_general(
                part, cb[k].reshape(2 * hr, LANES), tn, preferred_element_type=F32).astype(BF16)
        product = jnp.dot(og[...], qg[...].reshape(n * LANES, width), preferred_element_type=F32)
        ub[rows, :] = (tr[rows, :].astype(F32) - product).astype(BF16)
        return 0

    lax.fori_loop(0, tile // step, update, 0)
    w_up = local(4, ref(ub), ref(up_out))
    sent(f"fw{n - 1}")
    along(n - 1)

    second("pl", "pn", zv, rest)
    got("c0x", lambda: c0.at[:, oh], rest)
    all_in("zc", "pn", zv, rest)

    def same():
        q0g[...] = qg[...]
    on(first, same)
    blk = og0.shape[0]
    start = zz * 2 * sr
    lanes = pl.ds(pl.multiple_of(start // blk * blk, blk), blk)
    for k in range(n):
        part = xg[k, :, :, lanes].reshape(2 * hr, blk)
        og0[:, k * LANES:(k + 1) * LANES] = lax.dot_general(
            part, c0[k].reshape(2 * hr, LANES), tn, preferred_element_type=F32).astype(BF16)
    prod0[...] = jnp.dot(og0[...], q0g[...].reshape(n * LANES, width), preferred_element_type=F32)

    def finish(side, at):
        inside = pl.ds(pl.multiple_of(lax.rem(start, blk) + side * sr, sr), sr)
        nb[at] = (raw[side].astype(F32) - prod0[inside, :]).astype(BF16)

    def columns(side):
        return np_out.at[:, pl.ds(pl.multiple_of(side * width, width), width)]

    for w in w_raw:
        w()
    got("fw1", lambda: raw.at[oh], rest)
    finish(oh, 0)
    go("pfx", lambda: nb.at[0], lambda: columns(h), xn)
    got("ow1", lambda: raw.at[h], rest)
    finish(h, 1)
    w_np = local(8, lambda: nb.at[1], lambda: columns(h))
    got("pfx", lambda: columns(oh))
    for entry in pending:
        on(*entry[1:])
    w_up()
    w_np()


def body(trailing, left_outer, left_inner, upper_outer, upper_inner, left_ranks, upper_ranks):
    n = lax.axis_size("row")
    nc = lax.axis_size("col")
    tile, width = trailing.shape
    hr = left_outer.shape[0]
    sr = tile // nc
    blk = max(2 * sr, LANES)
    names = sem_names(n, n // 2)
    any_space = pl.BlockSpec(memory_space=pl.ANY)
    smem = pl.BlockSpec(memory_space=pltpu.SMEM)
    vmem = pltpu.VMEM
    return pl.pallas_call(
        functools.partial(kernel, n, names),
        out_shape=(
            jax.ShapeDtypeStruct((tile, width), BF16),
            jax.ShapeDtypeStruct((sr, 2 * width), BF16),
        ),
        in_specs=[any_space] * 5 + [smem] * 2,
        out_specs=(any_space, any_space),
        scratch_shapes=[
            vmem((n, 2, hr, tile), BF16),
            vmem((n, hr, tile), BF16),
            vmem((n, 2, LANES, width), BF16),
            vmem((n, LANES, width), BF16),
            vmem((n, LANES, width), BF16),
            vmem((n, 2, hr, LANES), BF16),
            vmem((n, 2, hr, LANES), BF16),
            vmem((256, n * LANES), BF16),
            vmem((blk, n * LANES), BF16),
            vmem((blk, width), F32),
            vmem((tile, width), BF16),
            vmem((tile, width), BF16),
            vmem((2, sr, width), BF16),
            vmem((2, sr, width), BF16),
            pltpu.SemaphoreType.DMA((len(names),)),
            pltpu.SemaphoreType.DMA((len(names),)),
            pltpu.SemaphoreType.DMA((9,)),
        ],
        compiler_params=pltpu.CompilerParams(
            collective_id=0, has_side_effects=True, vmem_limit_bytes=56 * 2 ** 20
        ),
        cost_estimate=pl.CostEstimate(
            flops=2 * tile * width * n * LANES, bytes_accessed=4 * tile * width, transcendentals=0
        ),
    )(trailing, left_outer, left_inner, upper_outer, upper_inner, left_ranks, upper_ranks)


def solution(mesh):
    in_specs = (
        P("row", "col"),
        P("col", "row"),
        P("col", "row"),
        P("row", "col"),
        P("row", "col"),
        P(),
        P(),
    )
    out_specs = (P("row", "col"), P(("row", "col"), None))
    return jax.shard_map(body, mesh=mesh, in_specs=in_specs, out_specs=out_specs, check_vma=False)
```

time: 44.5 us -> 52.5 us (1.18)
  Pallas kernels: 40.7 us -> 48.2 us
    pallas_call x1, Pallas kernels: 40.7 us -> 48.2 us  [body(): pl.pallas_call(functools.partial(kernel, n, names), out_shape=(jax.ShapeD...]
where the time goes in v4:
time: 52.5 us; the launch traced here: 51.8 us
  Pallas kernels  48.2 us (92%)
  local copies, waits for them, and re-layouts  3.01 us (6%)
  between operations  0.65 us (1%)
    pallas_call x1, Pallas kernels, body(): pl.pallas_call(functools.partial(kernel, n, names), out_shape=(jax.ShapeD...  48.2 us
    unnamed x4, local copies, waits for them, and re-layouts  3.01 us

profile of v4, /device:TPU:24, one launch (start us, length us, event | category | flops | bytes accessed | tf_op | source)
XLA Modules:
  0.0 51.8 jit_solution(725029397961507981)
XLA Ops:
  0.6 48.2 %shard_map.86 = (bf16[1024,512]{1,0:T(8,128)(2,1)}, bf16[128,1024]{1,0:T(8,128)(2,1)}) custom-call(bf16[1024,512]{1,0:T(8,128)(2,1)} %tr_in.1, bf16[48,1024]{1,0:T(8,128)(2,1)} %x_in.1, bf16[48,1024]{1,0:T(8,128)(2,1)} %y_in.1, bf16[96,512]{1,0:T(8,128)(2,1)} %p_in.1, bf16[96,512]{1,0:T(8,128)(2,1)} %q_in.1, s32[4,4]{1,0:T(4,128)} %lr.1, s32[4,4]{1,0:T(4,128)} %ur.1), custom_call_target="tpu_custom_call" | custom-call | flops 536870912 | bytes 2097152 | tf_op jit(solution)/shard_map/pallas_call | solution.py:311
  48.8 0.0 copy-start
  48.8 2.3 %copy.11 = bf16[1024,512]{1,0:T(8,128)(2,1)} copy(bf16[1024,512]{1,0:T(8,128)(2,1)} %get-tuple-element.4) | data formatting | bytes 2097152
  51.1 0.0 copy-done
  51.1 0.7 %copy.12 = bf16[128,1024]{1,0:T(8,128)(2,1)} copy(bf16[128,1024]{1,0:T(8,128)(2,1)S(1)} %copy-done) | data formatting | bytes 524288
Async XLA Ops:
  48.8 2.3 %copy-start = (bf16[128,1024]{1,0:T(8,128)(2,1)S(1)}, bf16[128,1024]{1,0:T(8,128)(2,1)}, u32[]{:S(2)}) copy-start(bf16[128,1024]{1,0:T(8,128)(2,1)} %get-tuple-element.5) | copy-start | bytes 786436

commit v5 on v4

--- a/solution.py
+++ b/solution.py
@@ -123,6 +123,7 @@
 
     go("yb1", ref(y_in), lambda: yv(zz), up, has_up)
     go("ya1", ref(y_in), lambda: yv(zz), down, has_down)
+    go("xb1", ref(x_in), lambda: xv(zz), up, first)
     go("px", ref(p_in), lambda: pv(h)(row), xn)
     spread("p1", "pg", pv(h), ref(p_in))
     w_p = local(0, ref(p_in), lambda: pv(h)(row))
@@ -166,17 +167,17 @@
                 go(f"c{side}{s}", dst, dst, xn, ok)
 
     relay("y", 1, yv)
-    go("xb1", ref(x_in), lambda: xv(zz), up, first)
+    go("xb1", ref(x_in), lambda: xv(zz), up, middle)
+    go("xa1", ref(x_in), lambda: xv(zz), down, has_down)
+    go("x0", ref(x_in), lambda: xv(zz), xn)
     across(1)
     second("pg", "pi", pv(h))
     for s in range(2, n):
         relay("y", s, yv)
         if s == 2:
-            go("xb1", ref(x_in), lambda: xv(zz), up, middle)
-            go("xa1", ref(x_in), lambda: xv(zz), down, has_down)
-            go("x0", ref(x_in), lambda: xv(zz), xn)
             go("z1", ref(q_in), lambda: zv(row), up, first)
             along(1)
+            relay("x", 1, xv)
             second("ph", "pj", pv(oh))
     spread("q1", "pk", qv, ref(q_in))
     w_p()
@@ -196,7 +197,7 @@
         live = (t_at < lr[row, k]) & (u_at < ur[k, zz])
         cb[k, pl.ds(h, 1)] = jnp.where(live, value, 0.0).astype(BF16)[None]
     go("cx", lambda: cb.at[:, h], lambda: cb.at[:, h], xn)
-    relay("x", 1, xv)
+    relay("x", 2, xv)
     got("cx", lambda: cb.at[:, oh])
 
     def keep():
@@ -222,7 +223,6 @@
         go("c0x", half, half, xn, cond)
 
     first_column(middle, True)
-    relay("x", 2, xv)
     relay_core(middle, True)
     for s in range(3, n):
         relay("x", s, xv)
@@ -242,22 +242,19 @@
         got(f"cb{s}", lambda s=s: xg.at[lax.rem(zz - s + n, n), oh], zz - s >= 0)
         got(f"ca{s}", lambda s=s: xg.at[lax.rem(zz + s, n), oh], zz + s < n)
     w_tr()
-    step = 256
-
-    def update(at, _):
-        rows = pl.ds(pl.multiple_of(at * step, step), step)
+    step = og.shape[0]
+    for at in range(tile // step):
+        rows = slice(at * step, (at + 1) * step)
         for k in range(n):
             part = xg[k, :, :, rows].reshape(2 * hr, step)
             og[:, k * LANES:(k + 1) * LANES] = lax.dot_general(
                 part, cb[k].reshape(2 * hr, LANES), tn, preferred_element_type=F32).astype(BF16)
         product = jnp.dot(og[...], qg[...].reshape(n * LANES, width), preferred_element_type=F32)
         ub[rows, :] = (tr[rows, :].astype(F32) - product).astype(BF16)
-        return 0
-
-    lax.fori_loop(0, tile // step, update, 0)
+        if at == 0:
+            sent(f"fw{n - 1}")
+            along(n - 1)
     w_up = local(4, ref(ub), ref(up_out))
-    sent(f"fw{n - 1}")
-    along(n - 1)
 
     second("pl", "pn", zv, rest)
     got("c0x", lambda: c0.at[:, oh], rest)
@@ -324,7 +321,7 @@
             vmem((n, LANES, width), BF16),
             vmem((n, 2, hr, LANES), BF16),
             vmem((n, 2, hr, LANES), BF16),
-            vmem((256, n * LANES), BF16),
+            vmem((512, n * LANES), BF16),
             vmem((blk, n * LANES), BF16),
             vmem((blk, width), F32),
             vmem((tile, width), BF16),

time: 52.5 us -> 49.6 us (0.945)
  Pallas kernels: 48.2 us -> 45.7 us
    pallas_call x1, Pallas kernels: 48.2 us -> 45.7 us  [body(): pl.pallas_call(functools.partial(kernel, n, names), out_shape=(jax.ShapeD...]
where the time goes in v5:
time: 49.6 us; the launch traced here: 49.4 us
  Pallas kernels  45.7 us (92%)
  local copies, waits for them, and re-layouts  3.01 us (6%)
  between operations  0.65 us (1%)
    pallas_call x1, Pallas kernels, body(): pl.pallas_call(functools.partial(kernel, n, names), out_shape=(jax.ShapeD...  45.7 us
    unnamed x4, local copies, waits for them, and re-layouts  3.01 us

profile of v5, /device:TPU:24, one launch (start us, length us, event | category | flops | bytes accessed | tf_op | source)
XLA Modules:
  0.0 49.4 jit_solution(2214021404770024696)
XLA Ops:
  0.6 45.7 %shard_map.86 = (bf16[1024,512]{1,0:T(8,128)(2,1)}, bf16[128,1024]{1,0:T(8,128)(2,1)}) custom-call(bf16[1024,512]{1,0:T(8,128)(2,1)} %tr_in.1, bf16[48,1024]{1,0:T(8,128)(2,1)} %x_in.1, bf16[48,1024]{1,0:T(8,128)(2,1)} %y_in.1, bf16[96,512]{1,0:T(8,128)(2,1)} %p_in.1, bf16[96,512]{1,0:T(8,128)(2,1)} %q_in.1, s32[4,4]{1,0:T(4,128)} %lr.1, s32[4,4]{1,0:T(4,128)} %ur.1), custom_call_target="tpu_custom_call" | custom-call | flops 536870912 | bytes 2097152 | tf_op jit(solution)/shard_map/pallas_call | solution.py:308
  46.4 0.0 copy-start
  46.4 2.3 %copy.11 = bf16[1024,512]{1,0:T(8,128)(2,1)} copy(bf16[1024,512]{1,0:T(8,128)(2,1)} %get-tuple-element.4) | data formatting | bytes 2097152
  48.7 0.0 copy-done
  48.7 0.7 %copy.12 = bf16[128,1024]{1,0:T(8,128)(2,1)} copy(bf16[128,1024]{1,0:T(8,128)(2,1)S(1)} %copy-done) | data formatting | bytes 524288
Async XLA Ops:
  46.4 2.3 %copy-start = (bf16[128,1024]{1,0:T(8,128)(2,1)S(1)}, bf16[128,1024]{1,0:T(8,128)(2,1)}, u32[]{:S(2)}) copy-start(bf16[128,1024]{1,0:T(8,128)(2,1)} %get-tuple-element.5) | copy-start | bytes 786436

commit v6 on v5

--- a/solution.py
+++ b/solution.py
@@ -64,11 +64,6 @@
         on(cond, lambda: make().start())
         pending.append((name, cond, lambda: make().wait_send()))
 
-    def sent(name):
-        for entry in [e for e in pending if e[0] == name]:
-            on(*entry[1:])
-            pending.remove(entry)
-
     def got(name, dst, cond=None):
         on(cond, lambda: desc(name, dst, dst, xn).wait_recv())
 
@@ -170,15 +165,35 @@
     go("xb1", ref(x_in), lambda: xv(zz), up, middle)
     go("xa1", ref(x_in), lambda: xv(zz), down, has_down)
     go("x0", ref(x_in), lambda: xv(zz), xn)
-    across(1)
+    go("z1", ref(q_in), lambda: zv(row), up, first)
+    across(n - 1)
     second("pg", "pi", pv(h))
+    def first_column(cond, more):
+        got("z1", lambda: zv(row), cond)
+        if more:
+            go("z1", lambda: zv(row), lambda: zv(row), up, cond)
+        go("zc", lambda: zv(row), lambda: zv(row), near, cond)
+        for d, dev in fars:
+            go(f"pl{d}", lambda: zv(row), lambda: zv(row), dev, cond)
+
+    half = lambda: c0.at[:, h]
+
+    def relay_core(cond, more):
+        got("c0", half, cond)
+        if more:
+            go("c0", half, half, up, cond)
+        go("c0x", half, half, xn, cond)
+
     for s in range(2, n):
         relay("y", s, yv)
         if s == 2:
-            go("z1", ref(q_in), lambda: zv(row), up, first)
-            along(1)
+            across(1)
+            along(n - 1)
             relay("x", 1, xv)
+            first_column(middle, True)
             second("ph", "pj", pv(oh))
+    for s in range(n - 2, 1, -1):
+        across(s)
     spread("q1", "pk", qv, ref(q_in))
     w_p()
     w_y()
@@ -197,42 +212,21 @@
         live = (t_at < lr[row, k]) & (u_at < ur[k, zz])
         cb[k, pl.ds(h, 1)] = jnp.where(live, value, 0.0).astype(BF16)[None]
     go("cx", lambda: cb.at[:, h], lambda: cb.at[:, h], xn)
-    relay("x", 2, xv)
     got("cx", lambda: cb.at[:, oh])
 
     def keep():
         c0[...] = cb[...]
     on(first, keep)
-    half = lambda: c0.at[:, h]
     go("c0", half, half, up, first)
-    if n > 2:
-        across(2)
-
-    def first_column(cond, more):
-        got("z1", lambda: zv(row), cond)
-        if more:
-            go("z1", lambda: zv(row), lambda: zv(row), up, cond)
-        go("zc", lambda: zv(row), lambda: zv(row), near, cond)
-        for d, dev in fars:
-            go(f"pl{d}", lambda: zv(row), lambda: zv(row), dev, cond)
-
-    def relay_core(cond, more):
-        got("c0", half, cond)
-        if more:
-            go("c0", half, half, up, cond)
-        go("c0x", half, half, xn, cond)
-
-    first_column(middle, True)
+    for s in range(n - 2, 1, -1):
+        along(s)
+    relay("x", 2, xv)
     relay_core(middle, True)
     for s in range(3, n):
         relay("x", s, xv)
-        across(s)
+    along(1)
     first_column(last, False)
     second("pk", "pm", qv)
-    for s in range(2, n - 1):
-        sent(f"fw{s}")
-        along(s)
-    relay_core(last, False)
 
     all_in("q1", "pm", qv)
     w_q()
@@ -251,11 +245,9 @@
                 part, cb[k].reshape(2 * hr, LANES), tn, preferred_element_type=F32).astype(BF16)
         product = jnp.dot(og[...], qg[...].reshape(n * LANES, width), preferred_element_type=F32)
         ub[rows, :] = (tr[rows, :].astype(F32) - product).astype(BF16)
-        if at == 0:
-            sent(f"fw{n - 1}")
-            along(n - 1)
     w_up = local(4, ref(ub), ref(up_out))
 
+    relay_core(last, False)
     second("pl", "pn", zv, rest)
     got("c0x", lambda: c0.at[:, oh], rest)
     all_in("zc", "pn", zv, rest)

time: 49.6 us -> 54 us (1.089)
  Pallas kernels: 45.7 us -> 49.9 us
    pallas_call x1, Pallas kernels: 45.7 us -> 49.9 us  [body(): pl.pallas_call(functools.partial(kernel, n, names), out_shape=(jax.ShapeD...]
where the time goes in v6:
time: 54 us; the launch traced here: 53.6 us
  Pallas kernels  49.9 us (92%)
  local copies, waits for them, and re-layouts  3.01 us (6%)
  between operations  0.65 us (1%)
    pallas_call x1, Pallas kernels, body(): pl.pallas_call(functools.partial(kernel, n, names), out_shape=(jax.ShapeD...  49.9 us
    unnamed x4, local copies, waits for them, and re-layouts  3.01 us

profile of v6, /device:TPU:24, one launch (start us, length us, event | category | flops | bytes accessed | tf_op | source)
XLA Modules:
  0.0 53.6 jit_solution(477820637524202419)
XLA Ops:
  0.6 49.9 %shard_map.86 = (bf16[1024,512]{1,0:T(8,128)(2,1)}, bf16[128,1024]{1,0:T(8,128)(2,1)}) custom-call(bf16[1024,512]{1,0:T(8,128)(2,1)} %tr_in.1, bf16[48,1024]{1,0:T(8,128)(2,1)} %x_in.1, bf16[48,1024]{1,0:T(8,128)(2,1)} %y_in.1, bf16[96,512]{1,0:T(8,128)(2,1)} %p_in.1, bf16[96,512]{1,0:T(8,128)(2,1)} %q_in.1, s32[4,4]{1,0:T(4,128)} %lr.1, s32[4,4]{1,0:T(4,128)} %ur.1), custom_call_target="tpu_custom_call" | custom-call | flops 536870912 | bytes 2097152 | tf_op jit(solution)/shard_map/pallas_call | solution.py:300
  50.6 0.0 copy-start
  50.6 2.3 %copy.11 = bf16[1024,512]{1,0:T(8,128)(2,1)} copy(bf16[1024,512]{1,0:T(8,128)(2,1)} %get-tuple-element.4) | data formatting | bytes 2097152
  52.9 0.0 copy-done
  52.9 0.7 %copy.12 = bf16[128,1024]{1,0:T(8,128)(2,1)} copy(bf16[128,1024]{1,0:T(8,128)(2,1)S(1)} %copy-done) | data formatting | bytes 524288
Async XLA Ops:
  50.6 2.3 %copy-start = (bf16[128,1024]{1,0:T(8,128)(2,1)S(1)}, bf16[128,1024]{1,0:T(8,128)(2,1)}, u32[]{:S(2)}) copy-start(bf16[128,1024]{1,0:T(8,128)(2,1)} %get-tuple-element.5) | copy-start | bytes 786436

commit v7 on v6

--- a/solution.py
+++ b/solution.py
@@ -118,7 +118,8 @@
 
     go("yb1", ref(y_in), lambda: yv(zz), up, has_up)
     go("ya1", ref(y_in), lambda: yv(zz), down, has_down)
-    go("xb1", ref(x_in), lambda: xv(zz), up, first)
+    go("xb1", ref(x_in), lambda: xv(zz), up, has_up)
+    go("xa1", ref(x_in), lambda: xv(zz), down, has_down)
     go("px", ref(p_in), lambda: pv(h)(row), xn)
     spread("p1", "pg", pv(h), ref(p_in))
     w_p = local(0, ref(p_in), lambda: pv(h)(row))
@@ -147,6 +148,7 @@
     on(rest, pad_first)
 
     got("px", lambda: pv(oh)(row))
+    go("x0", ref(x_in), lambda: xv(zz), xn)
     spread("q1p", "ph", pv(oh))
 
     def relay(nm, s, view):
@@ -161,12 +163,11 @@
             if nm == "x":
                 go(f"c{side}{s}", dst, dst, xn, ok)
 
+    spread("q1", "pk", qv, ref(q_in))
     relay("y", 1, yv)
-    go("xb1", ref(x_in), lambda: xv(zz), up, middle)
-    go("xa1", ref(x_in), lambda: xv(zz), down, has_down)
-    go("x0", ref(x_in), lambda: xv(zz), xn)
+    relay("x", 1, xv)
     go("z1", ref(q_in), lambda: zv(row), up, first)
-    across(n - 1)
+    across(1)
     second("pg", "pi", pv(h))
     def first_column(cond, more):
         got("z1", lambda: zv(row), cond)
@@ -186,15 +187,12 @@
 
     for s in range(2, n):
         relay("y", s, yv)
+        relay("x", s, xv)
         if s == 2:
-            across(1)
-            along(n - 1)
-            relay("x", 1, xv)
+            along(1)
+            second("ph", "pj", pv(oh))
             first_column(middle, True)
-            second("ph", "pj", pv(oh))
-    for s in range(n - 2, 1, -1):
-        across(s)
-    spread("q1", "pk", qv, ref(q_in))
+    across(2)
     w_p()
     w_y()
     all_in("p1", "pi", pv(h))
@@ -218,13 +216,10 @@
         c0[...] = cb[...]
     on(first, keep)
     go("c0", half, half, up, first)
-    for s in range(n - 2, 1, -1):
+    relay_core(middle, True)
+    for s in range(2, n - 1):
         along(s)
-    relay("x", 2, xv)
-    relay_core(middle, True)
-    for s in range(3, n):
-        relay("x", s, xv)
-    along(1)
+        across(s + 1)
     first_column(last, False)
     second("pk", "pm", qv)
 
@@ -245,6 +240,8 @@
                 part, cb[k].reshape(2 * hr, LANES), tn, preferred_element_type=F32).astype(BF16)
         product = jnp.dot(og[...], qg[...].reshape(n * LANES, width), preferred_element_type=F32)
         ub[rows, :] = (tr[rows, :].astype(F32) - product).astype(BF16)
+        if at == 0:
+            along(n - 1)
     w_up = local(4, ref(ub), ref(up_out))
 
     relay_core(last, False)

time: 54 us -> 47.8 us (0.89)
  Pallas kernels: 49.9 us -> 44 us
    pallas_call x1, Pallas kernels: 49.9 us -> 44 us  [body(): pl.pallas_call(functools.partial(kernel, n, names), out_shape=(jax.ShapeD...]
where the time goes in v7:
time: 47.8 us; the launch traced here: 47.6 us
  Pallas kernels  44 us (92%)
  local copies, waits for them, and re-layouts  3.01 us (6%)
  between operations  0.65 us (1%)
    pallas_call x1, Pallas kernels, body(): pl.pallas_call(functools.partial(kernel, n, names), out_shape=(jax.ShapeD...  44 us
    unnamed x4, local copies, waits for them, and re-layouts  3.01 us

profile of v7, /device:TPU:24, one launch (start us, length us, event | category | flops | bytes accessed | tf_op | source)
XLA Modules:
  0.0 47.6 jit_solution(1003425191920848229)
XLA Ops:
  0.6 44.0 %shard_map.86 = (bf16[1024,512]{1,0:T(8,128)(2,1)}, bf16[128,1024]{1,0:T(8,128)(2,1)}) custom-call(bf16[1024,512]{1,0:T(8,128)(2,1)} %tr_in.1, bf16[48,1024]{1,0:T(8,128)(2,1)} %x_in.1, bf16[48,1024]{1,0:T(8,128)(2,1)} %y_in.1, bf16[96,512]{1,0:T(8,128)(2,1)} %p_in.1, bf16[96,512]{1,0:T(8,128)(2,1)} %q_in.1, s32[4,4]{1,0:T(4,128)} %lr.1, s32[4,4]{1,0:T(4,128)} %ur.1), custom_call_target="tpu_custom_call" | custom-call | flops 536870912 | bytes 2097152 | tf_op jit(solution)/shard_map/pallas_call | solution.py:297
  44.6 0.0 copy-start
  44.6 2.3 %copy.11 = bf16[1024,512]{1,0:T(8,128)(2,1)} copy(bf16[1024,512]{1,0:T(8,128)(2,1)} %get-tuple-element.4) | data formatting | bytes 2097152
  46.9 0.0 copy-done
  46.9 0.7 %copy.12 = bf16[128,1024]{1,0:T(8,128)(2,1)} copy(bf16[128,1024]{1,0:T(8,128)(2,1)S(1)} %copy-done) | data formatting | bytes 524288
Async XLA Ops:
  44.6 2.3 %copy-start = (bf16[128,1024]{1,0:T(8,128)(2,1)S(1)}, bf16[128,1024]{1,0:T(8,128)(2,1)}, u32[]{:S(2)}) copy-start(bf16[128,1024]{1,0:T(8,128)(2,1)} %get-tuple-element.5) | copy-start | bytes 786436

commit v8 on v7

--- a/solution.py
+++ b/solution.py
@@ -14,10 +14,10 @@
 
 
 def sem_names(n, nh):
-    names = ["px", "x0", "q1", "p1", "q1p", "z1", "zc", "cx", "c0", "c0x", "pfx"]
+    names = ["px", "x0", "q1", "p1", "q1p", "z1", "zc", "cx", "c0x", "pfx"]
     for s in range(1, n):
         names += [f"xb{s}", f"xa{s}", f"yb{s}", f"ya{s}", f"cb{s}", f"ca{s}"]
-        names += [f"fw{s}", f"ow{s}"]
+        names += [f"fw{s}", f"ow{s}", f"cz{s}"]
     for d in range(1, nh):
         names += [f"p{a}{d}" for a in "ghijklmn"]
     return {name: at for at, name in enumerate(names)}
@@ -179,12 +179,6 @@
 
     half = lambda: c0.at[:, h]
 
-    def relay_core(cond, more):
-        got("c0", half, cond)
-        if more:
-            go("c0", half, half, up, cond)
-        go("c0x", half, half, xn, cond)
-
     for s in range(2, n):
         relay("y", s, yv)
         relay("x", s, xv)
@@ -192,7 +186,6 @@
             along(1)
             second("ph", "pj", pv(oh))
             first_column(middle, True)
-    across(2)
     w_p()
     w_y()
     all_in("p1", "pi", pv(h))
@@ -215,13 +208,17 @@
     def keep():
         c0[...] = cb[...]
     on(first, keep)
-    go("c0", half, half, up, first)
-    relay_core(middle, True)
-    for s in range(2, n - 1):
-        along(s)
-        across(s + 1)
+    for s in range(n - 1, 0, -1):
+        go(f"cz{s}", half, half, (row, s * 2 + h), first, "cz1")
+    for s in range(2, n):
+        across(s)
+        if s < n - 1:
+            along(s)
     first_column(last, False)
     second("pk", "pm", qv)
+    got("cz1", half, rest)
+    go("c0x", half, half, xn, rest)
+    second("pl", "pn", zv, rest)
 
     all_in("q1", "pm", qv)
     w_q()
@@ -244,8 +241,6 @@
             along(n - 1)
     w_up = local(4, ref(ub), ref(up_out))
 
-    relay_core(last, False)
-    second("pl", "pn", zv, rest)
     got("c0x", lambda: c0.at[:, oh], rest)
     all_in("zc", "pn", zv, rest)
 

time: 47.8 us -> 44.2 us (0.925)
  Pallas kernels: 44 us -> 40.3 us
    pallas_call x1, Pallas kernels: 44 us -> 40.3 us  [body(): pl.pallas_call(functools.partial(kernel, n, names), out_shape=(jax.ShapeD...]
where the time goes in v8:
time: 44.2 us; the launch traced here: 44 us
  Pallas kernels  40.3 us (91%)
  local copies, waits for them, and re-layouts  3.01 us (7%)
  between operations  0.65 us (1%)
    pallas_call x1, Pallas kernels, body(): pl.pallas_call(functools.partial(kernel, n, names), out_shape=(jax.ShapeD...  40.3 us
    unnamed x4, local copies, waits for them, and re-layouts  3.01 us

profile of v8, /device:TPU:24, one launch (start us, length us, event | category | flops | bytes accessed | tf_op | source)
XLA Modules:
  0.0 44.0 jit_solution(6682971122755620031)
XLA Ops:
  0.6 40.3 %shard_map.86 = (bf16[1024,512]{1,0:T(8,128)(2,1)}, bf16[128,1024]{1,0:T(8,128)(2,1)}) custom-call(bf16[1024,512]{1,0:T(8,128)(2,1)} %tr_in.1, bf16[48,1024]{1,0:T(8,128)(2,1)} %x_in.1, bf16[48,1024]{1,0:T(8,128)(2,1)} %y_in.1, bf16[96,512]{1,0:T(8,128)(2,1)} %p_in.1, bf16[96,512]{1,0:T(8,128)(2,1)} %q_in.1, s32[4,4]{1,0:T(4,128)} %lr.1, s32[4,4]{1,0:T(4,128)} %ur.1), custom_call_target="tpu_custom_call" | custom-call | flops 536870912 | bytes 2097152 | tf_op jit(solution)/shard_map/pallas_call | solution.py:292
  41.0 0.0 copy-start
  41.0 2.3 %copy.11 = bf16[1024,512]{1,0:T(8,128)(2,1)} copy(bf16[1024,512]{1,0:T(8,128)(2,1)} %get-tuple-element.4) | data formatting | bytes 2097152
  43.3 0.0 copy-done
  43.3 0.7 %copy.12 = bf16[128,1024]{1,0:T(8,128)(2,1)} copy(bf16[128,1024]{1,0:T(8,128)(2,1)S(1)} %copy-done) | data formatting | bytes 524288
Async XLA Ops:
  41.0 2.3 %copy-start = (bf16[128,1024]{1,0:T(8,128)(2,1)S(1)}, bf16[128,1024]{1,0:T(8,128)(2,1)}, u32[]{:S(2)}) copy-start(bf16[128,1024]{1,0:T(8,128)(2,1)} %get-tuple-element.5) | copy-start | bytes 786436

commit v9 on v8

--- a/solution.py
+++ b/solution.py
@@ -186,6 +186,7 @@
             along(1)
             second("ph", "pj", pv(oh))
             first_column(middle, True)
+            across(2)
     w_p()
     w_y()
     all_in("p1", "pi", pv(h))
@@ -210,10 +211,9 @@
     on(first, keep)
     for s in range(n - 1, 0, -1):
         go(f"cz{s}", half, half, (row, s * 2 + h), first, "cz1")
-    for s in range(2, n):
-        across(s)
-        if s < n - 1:
-            along(s)
+    for s in range(2, n - 1):
+        along(s)
+        across(s + 1)
     first_column(last, False)
     second("pk", "pm", qv)
     got("cz1", half, rest)
@@ -278,6 +278,19 @@
     w_np()
 
 
+def hand_on(u_in, p_in, u_out, p_out, sems):
+    parts = sems.shape[0] - 1
+    size = u_in.shape[0] // parts
+    copies = [pltpu.make_async_copy(p_in, p_out, sems.at[parts])]
+    for i in range(parts):
+        rows = pl.ds(i * size, size)
+        copies.append(pltpu.make_async_copy(u_in.at[rows], u_out.at[rows], sems.at[i]))
+    for c in copies:
+        c.start()
+    for c in copies:
+        c.wait()
+
+
 def body(trailing, left_outer, left_inner, upper_outer, upper_inner, left_ranks, upper_ranks):
     n = lax.axis_size("row")
     nc = lax.axis_size("col")
@@ -289,12 +302,13 @@
     any_space = pl.BlockSpec(memory_space=pl.ANY)
     smem = pl.BlockSpec(memory_space=pltpu.SMEM)
     vmem = pltpu.VMEM
-    return pl.pallas_call(
+    shapes = (
+        jax.ShapeDtypeStruct((tile, width), BF16),
+        jax.ShapeDtypeStruct((sr, 2 * width), BF16),
+    )
+    results = pl.pallas_call(
         functools.partial(kernel, n, names),
-        out_shape=(
-            jax.ShapeDtypeStruct((tile, width), BF16),
-            jax.ShapeDtypeStruct((sr, 2 * width), BF16),
-        ),
+        out_shape=shapes,
         in_specs=[any_space] * 5 + [smem] * 2,
         out_specs=(any_space, any_space),
         scratch_shapes=[
@@ -323,6 +337,14 @@
             flops=2 * tile * width * n * LANES, bytes_accessed=4 * tile * width, transcendentals=0
         ),
     )(trailing, left_outer, left_inner, upper_outer, upper_inner, left_ranks, upper_ranks)
+    return pl.pallas_call(
+        hand_on,
+        out_shape=shapes,
+        in_specs=[any_space] * 2,
+        out_specs=(any_space, any_space),
+        scratch_shapes=[pltpu.SemaphoreType.DMA((9,))],
+        compiler_params=pltpu.CompilerParams(vmem_limit_bytes=56 * 2 ** 20),
+    )(*results)
 
 
 def solution(mesh):

time: 44.2 us -> 79.2 us (1.79)
  Pallas kernels: 40.3 us -> 78.4 us
  local copies, waits for them, and re-layouts: 3.01 us -> 0 us
    pallas_call x1 -> x2, Pallas kernels: 40.3 us -> 78.4 us  [the longest x1 40.9 us: body(): pl.pallas_call(hand_on, out_shape=shapes, in_specs=[any_space] * 2, out_s...]
    unnamed x4 -> x0, local copies, waits for them, and re-layouts: 3.01 us -> none
where the time goes in v9:
time: 79.2 us; the launch traced here: 79 us
  Pallas kernels  78.4 us (99%)
    pallas_call x1, Pallas kernels, body(): pl.pallas_call(hand_on, out_shape=shapes, in_specs=[any_space] * 2, out_s...  40.9 us
    pallas_call x1, Pallas kernels, body(): pl.pallas_call(functools.partial(kernel, n, names), out_shape=shapes, in_...  37.5 us

profile of v9, /device:TPU:24, one launch (start us, length us, event | category | flops | bytes accessed | tf_op | source)
XLA Modules:
  0.0 79.0 jit_solution(4302690713483620273)
XLA Ops:
  0.6 37.5 %shard_map.86 = (bf16[1024,512]{1,0:T(8,128)(2,1)}, bf16[128,1024]{1,0:T(8,128)(2,1)}) custom-call(bf16[1024,512]{1,0:T(8,128)(2,1)} %tr_in.1, bf16[48,1024]{1,0:T(8,128)(2,1)} %x_in.1, bf16[48,1024]{1,0:T(8,128)(2,1)} %y_in.1, bf16[96,512]{1,0:T(8,128)(2,1)} %p_in.1, bf16[96,512]{1,0:T(8,128)(2,1)} %q_in.1, s32[4,4]{1,0:T(4,128)} %lr.1, s32[4,4]{1,0:T(4,128)} %ur.1), custom_call_target="tpu_custom_call" | custom-call | flops 536870912 | bytes 2097152 | tf_op jit(solution)/shard_map/pallas_call | solution.py:309
  38.2 40.9 %shard_map.87 = (bf16[1024,512]{1,0:T(8,128)(2,1)}, bf16[128,1024]{1,0:T(8,128)(2,1)}) custom-call(bf16[1024,512]{1,0:T(8,128)(2,1)} %get-tuple-element.4.u_in, bf16[128,1024]{1,0:T(8,128)(2,1)} %get-tuple-element.5.p_in), custom_call_target="tpu_custom_call" | custom-call | tf_op jit(solution)/shard_map/pallas_call | solution.py:340

commit v10 on v9

--- a/solution.py
+++ b/solution.py
@@ -278,17 +278,22 @@
     w_np()
 
 
-def hand_on(u_in, p_in, u_out, p_out, sems):
-    parts = sems.shape[0] - 1
+def hand_on(u_in, p_in, u_out, p_out, u_buf, p_buf, sems):
+    parts = sems.shape[1] - 1
     size = u_in.shape[0] // parts
-    copies = [pltpu.make_async_copy(p_in, p_out, sems.at[parts])]
+    views = [(p_in, p_buf, p_out)]
     for i in range(parts):
         rows = pl.ds(i * size, size)
-        copies.append(pltpu.make_async_copy(u_in.at[rows], u_out.at[rows], sems.at[i]))
-    for c in copies:
+        views.append((u_in.at[rows], u_buf.at[rows], u_out.at[rows]))
+    ins = [pltpu.make_async_copy(v[0], v[1], sems.at[0, i]) for i, v in enumerate(views)]
+    outs = [pltpu.make_async_copy(v[1], v[2], sems.at[1, i]) for i, v in enumerate(views)]
+    for c in ins:
         c.start()
-    for c in copies:
+    for c, o in zip(ins, outs):
         c.wait()
+        o.start()
+    for o in outs:
+        o.wait()
 
 
 def body(trailing, left_outer, left_inner, upper_outer, upper_inner, left_ranks, upper_ranks):
@@ -342,7 +347,11 @@
         out_shape=shapes,
         in_specs=[any_space] * 2,
         out_specs=(any_space, any_space),
-        scratch_shapes=[pltpu.SemaphoreType.DMA((9,))],
+        scratch_shapes=[
+            vmem((tile, width), BF16),
+            vmem((sr, 2 * width), BF16),
+            pltpu.SemaphoreType.DMA((2, 5)),
+        ],
         compiler_params=pltpu.CompilerParams(vmem_limit_bytes=56 * 2 ** 20),
     )(*results)
 

time: 79.2 us -> 40.4 us (0.51)
  Pallas kernels: 78.4 us -> 39.6 us
    pallas_call x1, Pallas kernels: 40.9 us -> 2.08 us  [body(): pl.pallas_call(hand_on, out_shape=shapes, in_specs=[any_space] * 2, out_s...]
where the time goes in v10:
time: 40.4 us; the launch traced here: 40.2 us
  Pallas kernels  39.6 us (98%)
  between operations  0.64 us (2%)
    pallas_call x1, Pallas kernels, body(): pl.pallas_call(functools.partial(kernel, n, names), out_shape=shapes, in_...  37.5 us
    pallas_call x1, Pallas kernels, body(): pl.pallas_call(hand_on, out_shape=shapes, in_specs=[any_space] * 2, out_s...  2.08 us

profile of v10, /device:TPU:24, one launch (start us, length us, event | category | flops | bytes accessed | tf_op | source)
XLA Modules:
  0.0 40.2 jit_solution(5150571481764146512)
XLA Ops:
  0.6 37.5 %shard_map.86 = (bf16[1024,512]{1,0:T(8,128)(2,1)}, bf16[128,1024]{1,0:T(8,128)(2,1)}) custom-call(bf16[1024,512]{1,0:T(8,128)(2,1)} %tr_in.1, bf16[48,1024]{1,0:T(8,128)(2,1)} %x_in.1, bf16[48,1024]{1,0:T(8,128)(2,1)} %y_in.1, bf16[96,512]{1,0:T(8,128)(2,1)} %p_in.1, bf16[96,512]{1,0:T(8,128)(2,1)} %q_in.1, s32[4,4]{1,0:T(4,128)} %lr.1, s32[4,4]{1,0:T(4,128)} %ur.1), custom_call_target="tpu_custom_call" | custom-call | flops 536870912 | bytes 2097152 | tf_op jit(solution)/shard_map/pallas_call | solution.py:314
  38.2 2.1 %shard_map.87 = (bf16[1024,512]{1,0:T(8,128)(2,1)}, bf16[128,1024]{1,0:T(8,128)(2,1)}) custom-call(bf16[1024,512]{1,0:T(8,128)(2,1)} %get-tuple-element.4.u_in, bf16[128,1024]{1,0:T(8,128)(2,1)} %get-tuple-element.5.p_in), custom_call_target="tpu_custom_call" | custom-call | tf_op jit(solution)/shard_map/pallas_call | solution.py:345
